TPU v7x, 512 devices: a whole 4x8x8 slice. The times are simulated.
512 devices in a mesh: enc: 16 (over x, z_hi), lat: 4 (over z_lo, core), lon: 8 (over y).
Axes of the slice: x: 4, y: 8, z: 8 (z_hi: 4, z_lo: 2; z = z_hi * 2 + z_lo), core: 2. Of those that a mesh axis runs over, the one named last changes fastest.
Arguments:
- atmos: bfloat16 [96, 192, 13, 500], P('enc', ('lon', 'lat')), may hold values from -6 to 6
- land_sea: int32 [96, 192, 100], P('enc', ('lon', 'lat')), may hold values 0 or 1
- level_count: int32 [96, 192], P('enc', ('lon', 'lat')), may hold values from 8 to 13
- atm_weight: bfloat16 [500, 512], replicated, may hold values from -0.25 to 0.25
- land_weight: bfloat16 [100, 512], replicated, may hold values from -1.25 to 1.25
- level_embed: float32 [13, 512], replicated, may hold values from -6 to 6
- latent_query: bfloat16 [3, 512], replicated, may hold values from -6 to 6
- key_weight: bfloat16 [512, 512], replicated, may hold values from -0.25 to 0.25
- value_weight: bfloat16 [512, 512], replicated, may hold values from -0.25 to 0.25
- merge_weight: bfloat16 [2048, 1024], replicated, may hold values from -0.125 to 0.125
- lat_shift: int32 [1], replicated, may hold values from 1 to 5
- lon_shift: int32 [1], replicated, may hold values from 1 to 11
- qkv_weight: bfloat16 [1024, 3072], P(None, 'enc'), may hold values from -1 to 1
- proj_weight: bfloat16 [1024, 1024], P('enc'), may hold values from -0.75 to 0.75
- cotangent: bfloat16 [3, 48, 96, 1024], P(None, 'lat', 'lon'), may hold values from -6 to 6
Outputs:
- grad_latent: bfloat16 [3, 48, 96, 1024], P(None, 'lat', 'lon', 'enc')
- grad_qkv: float32 [1024, 3072], P(('lat', 'lon'), 'enc')
- grad_proj: float32 [1024, 1024], P('enc', ('lat', 'lon'))
Inputs may be any that keep to these rules, and one draw needn't show every extreme that they name: Levels 0 to level_count - 1 of a fine patch lie above ground; the others carry no data.
All inputs are finite; a program needn't handle non-finite values. No bound on the sum of `land_sea` on one device may be relied on, other than what follows from the above.
Results may differ from a plain program's by a relative error of at most 0.033.
Values may be sent and summed in bfloat16 or wider, within the bound.
A program may use at most 128 MiB of HBM per device.

v0:
```python
import jax
import jax.numpy as jnp
from jax import lax
from jax.sharding import PartitionSpec as P

PHEADS = 16
WIN_LAT = 6
WIN_LON = 12
HD = 64


epsilon = 1e-05


def padded(block, sides, width):
    for axis, dim in sides:
        count = lax.axis_size(axis)
        forward = [(i, i + 1) for i in range(count - 1)]
        forward.append((count - 1, 0))
        backward = [(target, source) for source, target in forward]
        low = lax.ppermute(
            lax.slice_in_dim(block, block.shape[dim] - width, None, axis=dim), axis, forward
        )
        high = lax.ppermute(lax.slice_in_dim(block, 0, width, axis=dim), axis, backward)
        block = jnp.concatenate([low, block, high], axis=dim)
    return block


def layer_norm(values):
    centre = jnp.mean(values, axis=-1, keepdims=True)
    centred = values - centre
    variance = jnp.mean(centred * centred, axis=-1, keepdims=True)
    inverse = lax.rsqrt(variance + epsilon)
    return (centred * inverse, inverse)


def encode(
    atmos,
    land_sea,
    level_count,
    atm_weight,
    land_weight,
    level_embed,
    latent_query,
    key_weight,
    value_weight,
):
    row_count, col_count, levels, pixels = atmos.shape
    patches = row_count * col_count
    embedded = jnp.dot(
        atmos.reshape(patches * levels, pixels), atm_weight, preferred_element_type=jnp.float32
    )
    embedded = embedded.reshape(patches, levels, -1)
    static = jnp.dot(
        land_sea.reshape(patches, -1).astype(jnp.bfloat16),
        land_weight,
        preferred_element_type=jnp.float32,
    )
    embedded = embedded + level_embed[None, :, :] + static[:, None, :]
    normed, unused_scale = layer_norm(embedded)
    tokens = normed.astype(jnp.bfloat16).reshape(patches * levels, -1)
    key_rows = jnp.dot(tokens, key_weight, preferred_element_type=jnp.float32).astype(jnp.bfloat16)
    value_rows = jnp.dot(tokens, value_weight, preferred_element_type=jnp.float32).astype(
        jnp.bfloat16
    )
    key_rows = key_rows.reshape(patches, levels, PHEADS, -1)
    value_rows = value_rows.reshape(patches, levels, PHEADS, -1)
    queries = latent_query.reshape(latent_query.shape[0], PHEADS, -1)
    score_scale = key_rows.shape[-1] ** (-0.5)
    scores = (
        jnp.einsum("mhc,plhc->phml", queries, key_rows, preferred_element_type=jnp.float32)
        * score_scale
    )
    present = jnp.arange(levels, dtype=jnp.int32)[None, :] < level_count.reshape(patches, 1)
    weights = jnp.where(present[:, None, None, :], jnp.exp(scores), 0.0)
    level_probs = (weights / jnp.sum(weights, axis=-1, keepdims=True)).astype(jnp.bfloat16)
    attended = jnp.einsum(
        "phml,plhc->pmhc", level_probs, value_rows, preferred_element_type=jnp.float32
    )
    attended = attended.astype(jnp.bfloat16).reshape(row_count, col_count, queries.shape[0], -1)
    return attended.transpose(2, 0, 1, 3)


def merge_patches(fine, merge_weight):
    levels, row_count, col_count, width = fine.shape
    grouped = fine.reshape(levels, row_count // 2, 2, col_count // 2, 2, width).transpose(
        0, 1, 3, 4, 2, 5
    )
    grouped = grouped.reshape(levels, row_count // 2, col_count // 2, 4 * width)
    merge_in = layer_norm(grouped.astype(jnp.float32))[0].astype(jnp.bfloat16)
    merged = jnp.dot(
        merge_in.reshape(-1, 4 * width), merge_weight, preferred_element_type=jnp.float32
    ).astype(jnp.bfloat16)
    return merged.reshape(levels, row_count // 2, col_count // 2, -1)


def split_windows(field, head_count):
    levels, row_count, col_count, unused = field.shape
    pieces = field.reshape(
        levels, row_count // WIN_LAT, WIN_LAT, col_count // WIN_LON, WIN_LON, head_count, -1
    )
    pieces = pieces.transpose(1, 3, 5, 0, 2, 4, 6)
    return pieces.reshape(
        row_count // WIN_LAT, col_count // WIN_LON, head_count, levels * WIN_LAT * WIN_LON, -1
    )


def join_windows(pieces, levels):
    row_windows, col_windows, head_count, unused, channels = pieces.shape
    field = pieces.reshape(row_windows, col_windows, head_count, levels, WIN_LAT, WIN_LON, channels)
    field = field.transpose(3, 0, 4, 1, 5, 2, 6)
    return field.reshape(
        levels, row_windows * WIN_LAT, col_windows * WIN_LON, head_count * channels
    )


def token_sides(row_sides, levels):
    row_windows = row_sides.shape[0] // WIN_LAT
    token_side = jnp.broadcast_to(
        row_sides.reshape(row_windows, 1, WIN_LAT, 1), (row_windows, levels, WIN_LAT, WIN_LON)
    )
    return token_side.reshape(row_windows, levels * WIN_LAT * WIN_LON)


def window_pass(qkv_win, grad_win, side_win):
    head_dim = grad_win.shape[-1]
    queries = qkv_win[..., :head_dim]
    key_part = qkv_win[..., head_dim : 2 * head_dim]
    value_part = qkv_win[..., 2 * head_dim :]
    score_scale = head_dim ** (-0.5)
    scores = (
        jnp.einsum("...td,...ud->...tu", queries, key_part, preferred_element_type=jnp.float32)
        * score_scale
    )
    same_side = side_win[..., :, None] == side_win[..., None, :]
    weights = jnp.where(same_side, jnp.exp(scores), 0.0)
    probs = weights / jnp.sum(weights, axis=-1, keepdims=True)
    probs_low = probs.astype(jnp.bfloat16)
    heads_out = jnp.einsum(
        "...tu,...ud->...td", probs_low, value_part, preferred_element_type=jnp.float32
    ).astype(jnp.bfloat16)
    grad_probs = jnp.einsum(
        "...td,...ud->...tu", grad_win, value_part, preferred_element_type=jnp.float32
    )
    grad_values = jnp.einsum(
        "...tu,...td->...ud", probs_low, grad_win, preferred_element_type=jnp.float32
    ).astype(jnp.bfloat16)
    grad_scores = probs * (grad_probs - jnp.sum(grad_probs * probs, axis=-1, keepdims=True))
    grad_low = grad_scores.astype(jnp.bfloat16)
    grad_query = (
        jnp.einsum("...tu,...ud->...td", grad_low, key_part, preferred_element_type=jnp.float32)
        * score_scale
    ).astype(jnp.bfloat16)
    grad_keys = (
        jnp.einsum("...tu,...td->...ud", grad_low, queries, preferred_element_type=jnp.float32)
        * score_scale
    ).astype(jnp.bfloat16)
    return (heads_out, jnp.concatenate([grad_query, grad_keys, grad_values], axis=-1))


def window_region(field, row_shift, col_shift):
    levels, tile_rows, tile_cols, channels = field.shape
    widened = padded(field, (("lon", 2),), WIN_LON - 1)
    extended = padded(widened, (("lat", 1),), WIN_LAT - 1)
    anchor = (jnp.int32(0), WIN_LAT - 1 - row_shift, WIN_LON - 1 - col_shift, jnp.int32(0))
    return lax.dynamic_slice(
        extended, anchor, (levels, tile_rows + WIN_LAT, tile_cols + WIN_LON, channels)
    )


def local(
    atmos,
    land_sea,
    level_count,
    atm_weight,
    land_weight,
    level_embed,
    latent_query,
    key_weight,
    value_weight,
    merge_weight,
    lat_shift,
    lon_shift,
    qkv_weight,
    proj_weight,
    cotangent,
):
    fine_band = encode(
        atmos,
        land_sea,
        level_count,
        atm_weight,
        land_weight,
        level_embed,
        latent_query,
        key_weight,
        value_weight,
    )
    latent_band = merge_patches(fine_band, merge_weight)
    enc_count = lax.axis_size("enc")
    lat_count = lax.axis_size("lat")
    lon_count = lax.axis_size("lon")
    levels, band_height, block_width, feature_count = latent_band.shape
    column_rows = lax.all_gather(latent_band, "enc", axis=1, tiled=True)
    latents = lax.all_to_all(column_rows, "lat", split_axis=1, concat_axis=2, tiled=True)
    tile_rows = latents.shape[1]
    tile_cols = latents.shape[2]
    row_shift = lat_shift[0]
    col_shift = lon_shift[0]
    normed, inverse = layer_norm(latents.astype(jnp.float32))
    hidden = normed.astype(jnp.bfloat16)
    local_heads = proj_weight.shape[0] // HD
    hidden_region = window_region(hidden, row_shift, col_shift)
    qkv_region = jnp.dot(hidden_region, qkv_weight, preferred_element_type=jnp.float32).astype(
        jnp.bfloat16
    )
    head_grad = jnp.einsum(
        "lrcd,hd->lrch", cotangent, proj_weight, preferred_element_type=jnp.float32
    ).astype(jnp.bfloat16)
    grad_region = window_region(head_grad, row_shift, col_shift)
    total_rows = tile_rows * lat_count
    region_rows = (
        jnp.arange(tile_rows + WIN_LAT, dtype=jnp.int32) + lax.axis_index("lat") * tile_rows
    )
    row_sides = region_rows % total_rows < row_shift
    side_win = token_sides(row_sides, levels)[:, None, None, :]
    out_win, dqkv_win = window_pass(
        split_windows(qkv_region, local_heads), split_windows(grad_region, local_heads), side_win
    )
    out_region = join_windows(out_win, levels)
    dqkv_region = join_windows(dqkv_win, levels)
    anchor = (jnp.int32(0), row_shift, col_shift, jnp.int32(0))
    heads_out = lax.dynamic_slice(
        out_region, anchor, (levels, tile_rows, tile_cols, out_region.shape[3])
    )
    grad_rows = lax.dynamic_slice(
        dqkv_region, anchor, (levels, tile_rows, tile_cols, dqkv_region.shape[3])
    )
    factor = (levels * tile_rows * tile_cols * lat_count * lon_count) ** (-0.5)
    contract_rows = (((0,), (0,)), ((), ()))
    grad_qkv_part = (
        lax.dot_general(
            hidden.reshape(-1, feature_count),
            grad_rows.reshape(-1, grad_rows.shape[3]),
            contract_rows,
            preferred_element_type=jnp.float32,
        )
        * factor
    )
    grad_proj_part = (
        lax.dot_general(
            heads_out.reshape(-1, heads_out.shape[3]),
            cotangent.reshape(-1, feature_count),
            contract_rows,
            preferred_element_type=jnp.float32,
        )
        * factor
    )
    grad_qkv, grad_proj = (
        lax.psum_scatter(
            grad_qkv_part.astype(jnp.bfloat16), ("lat", "lon"), scatter_dimension=0, tiled=True
        ).astype(jnp.float32),
        lax.psum_scatter(
            grad_proj_part.astype(jnp.bfloat16), ("lat", "lon"), scatter_dimension=1, tiled=True
        ).astype(jnp.float32),
    )
    head_part = jnp.einsum(
        "lrcq,dq->lrcd", grad_rows, qkv_weight, preferred_element_type=jnp.float32
    )
    feature_sums = jnp.stack(
        [jnp.sum(head_part, axis=-1), jnp.sum(head_part * normed, axis=-1)], axis=-1
    )
    sums_wide = jnp.tile(feature_sums, (1, 1, 1, enc_count))
    head_slice, totals = (
        lax.psum_scatter(
            head_part.astype(jnp.bfloat16), "enc", scatter_dimension=3, tiled=True
        ).astype(jnp.float32),
        lax.psum_scatter(
            sums_wide.astype(jnp.bfloat16), "enc", scatter_dimension=3, tiled=True
        ).astype(jnp.float32),
    )
    share_width = feature_count // enc_count
    offset = lax.axis_index("enc") * share_width
    normed_slice = lax.dynamic_slice_in_dim(normed, offset, share_width, 3)
    cot_slice = lax.dynamic_slice_in_dim(cotangent, offset, share_width, 3).astype(jnp.float32)
    mean_grad = totals[..., 0:1] / feature_count
    mean_cross = totals[..., 1:2] / feature_count
    grad_latent = cot_slice + inverse * (head_slice - mean_grad - normed_slice * mean_cross)
    return (grad_latent.astype(jnp.bfloat16), grad_qkv, grad_proj)


def solution(mesh):
    return jax.shard_map(
        local,
        mesh=mesh,
        in_specs=(
            P("enc", ("lon", "lat"), None, None),
            P("enc", ("lon", "lat"), None),
            P("enc", ("lon", "lat")),
            P(),
            P(),
            P(),
            P(),
            P(),
            P(),
            P(),
            P(),
            P(),
            P(None, "enc"),
            P("enc", None),
            P(None, "lat", "lon", None),
        ),
        out_specs=(
            P(None, "lat", "lon", "enc"),
            P(("lat", "lon"), "enc"),
            P("enc", ("lat", "lon")),
        ),
        check_vma=False,
    )
```

profile of v0, /device:TPU:1, one launch (start us, length us, event | category | flops | bytes accessed | tf_op | source)
XLA Modules:
  0.0 684.8 jit_solution(18370694611567397750)
XLA Ops:
  15.8 2.6 reshape.256
  18.4 2.3 reshape.257
  20.7 3.9 fusion.92
  30.0 3.1 convolution_convert_fusion.5
  33.2 53.1 %all_gather.3 = bf16[3,48,3,1024]{3,2,0,1:T(4,128)(2,1)S(1)} all-gather(bf16[3,3,3,1024]{3,2,0,1:T(4,128)(2,1)S(1)} %copy.140), channel_id=1, replica_groups=mesh['enc'=16,'lat'=4,'lon'=8] {'enc'}, dimensions={1}, use_global_device_ids=true | all-gather | bytes 940032 | tf_op jit(solution)/shard_map/all_gather | solution.py:204
  86.3 25.9 %all_to_all.4 = bf16[3,48,3,1024]{3,2,0,1:T(4,128)(2,1)S(1)} all-to-all(bf16[3,48,3,1024]{3,2,0,1:T(4,128)(2,1)S(1)} %all_gather.3), channel_id=1, replica_groups=mesh['enc'=16,'lat'=4,'lon'=8] {'lat'}, dimensions={1} | all-to-all | bytes 1769472 | tf_op jit(solution)/shard_map/all_to_all | solution.py:205
  120.3 8.7 %collective-permute-start.1 = (bf16[3,12,11,1024]{3,1,2,0:T(8,128)(2,1)S(1)}, bf16[3,12,11,1024]{3,1,2,0:T(8,128)(2,1)S(1)}, u32[]{:S(2)}, u32[]{:S(2)}) collective-permute-start(bf16[3,12,11,1024]{3,1,2,0:T(8,128)(2,1)S(1)} %copy.150), channel_id=1, source_target_pairs={{1,0},{2,1},{3,2},{4,3},{5,4},{6,5},{7,6},{0,7},{9,8},{10,9},{11,1... | collective-permute-start | bytes 2433032 | tf_op jit(solution)/shard_map/ppermute | solution.py:24
  131.5 19.7 %collective-permute-done.1 = bf16[3,12,11,1024]{3,1,2,0:T(8,128)(2,1)S(1)} collective-permute-done((bf16[3,12,11,1024]{3,1,2,0:T(8,128)(2,1)S(1)}, bf16[3,12,11,1024]{3,1,2,0:T(8,128)(2,1)S(1)}, u32[]{:S(2)}, u32[]{:S(2)}) %collective-permute-start.1) | collective-permute-done | bytes 811040 | tf_op jit(solution)/shard_map/ppermute | solution.py:24
  151.6 5.1 collective-permute-done
  157.2 2.5 pad_maximum_fusion
  159.7 4.1 collective-permute-start.3
  163.8 2.3 collective-permute-start.2
  169.9 4.6 collective-permute-start.5
  179.6 3.1 collective-permute-start.7
  182.6 3.3 collective-permute-start.6
  187.4 5.6 collective-permute-done.7
  194.4 2.7 fusion.52
  202.8 9.1 %fusion.15 = bf16[3,18,24,192]{3,2,1,0:T(8,128)(2,1)} fusion(s32[]{:T(128)S(6)} %select_n.47, s32[]{:T(128)S(6)} %select_n.48, bf16[3,5,34,1024]{3,2,1,0:T(8,128)(2,1)} %collective-permute-done.2, bf16[3,12,11,1024]{3,2,1,0:T(8,128)(2,1)} %copy-done.5, bf16[3,12,12,1024]{3,2,1,0:T(8,128)(2,1)S(1)} %get-tuple-element.5, ...), kind=kOutput, calls=%fused_computation.25 | convolution fusion | flops 523127808 | bytes 5486600 | tf_op jit(solution)/shard_map/dot_general | solution.py:214
  211.9 2.3 reshape.261
  226.9 2.8 convolution_convert_fusion.2
  229.7 2.9 convolution_convert_fusion.3
  248.7 2.8 maximum_bitcast_fusion
  254.7 2.7 fusion.85
  258.3 2.7 fusion.41
  261.1 2.5 fusion.27
  263.6 14.2 %copy.181 = bf16[3,12,12,1024]{2,1,0,3:T(8,128)(2,1)} copy(bf16[3,12,12,1024]{3,2,1,0:T(8,128)(2,1)} %get-tuple-element.9) | data formatting | bytes 1769472
  277.9 14.1 %reshape.285 = bf16[1024,432]{1,0:T(8,128)(2,1)} reshape(bf16[1024,3,12,12]{3,2,1,0:T(8,128)(2,1)} %bitcast.144) | data formatting | bytes 1769472
  292.0 47.7 %reduce-scatter.7.cloned.1.call-done = bf16[3,12,12,2]{2,1,0,3:T(8,128)(2,1)} async-done(((bf16[3,12,12,32]{2,1,0,3:T(8,128)(2,1)}), bf16[3,12,12,2]{2,1,0,3:T(8,128)(2,1)}) %reduce-scatter.7.cloned.1.call-update) | async-done | bytes 1744 | tf_op jit(solution)/shard_map/reduce_scatter | solution.py:278
  340.5 116.7 %reduce-scatter.11.cloned.1.call-done = bf16[64,32]{0,1:T(8,128)(2,1)} async-done(((bf16[64,1024]{0,1:T(8,128)(2,1)}), bf16[64,32]{0,1:T(8,128)(2,1)}) %reduce-scatter.11.cloned.1.call-update) | async-done | bytes 4112 | tf_op jit(solution)/shard_map/reduce_scatter | solution.py:263
  458.6 117.9 %reduce-scatter.9.cloned.1.call-done = bf16[32,192]{1,0:T(8,128)(2,1)} async-done(((bf16[1024,192]{1,0:T(8,128)(2,1)}), bf16[32,192]{1,0:T(8,128)(2,1)}) %reduce-scatter.9.cloned.1.call-update) | async-done | bytes 12304 | tf_op jit(solution)/shard_map/reduce_scatter | solution.py:260
  577.8 94.1 %reduce-scatter.13.cloned.1.call-done = bf16[64,432]{1,0:T(8,128)(2,1)} async-done(((bf16[1024,432]{1,0:T(8,128)(2,1)}), bf16[64,432]{1,0:T(8,128)(2,1)}) %reduce-scatter.13.cloned.1.call-update) | async-done | bytes 55312
  671.9 2.4 reshape.286
  (132 shorter events, 81.6 us)
Async XLA Ops:
  7.2 6.2 copy-start
  7.2 332.5 %reduce-scatter.7.cloned.1.call-start = ((), (), s32[]{:S(2)}) async-start(), calls=%async_computation.5 | async-start | bytes 417792 | tf_op jit(solution)/shard_map/reduce_scatter | solution.py:278
  13.2 1.4 copy-start.11
  15.8 2.6 copy-start.7
  117.4 0.7 copy-start.12
  117.4 0.8 copy-start.15
  120.3 30.8 %collective-permute-start.1 = (bf16[3,12,11,1024]{3,1,2,0:T(8,128)(2,1)S(1)}, bf16[3,12,11,1024]{3,1,2,0:T(8,128)(2,1)S(1)}, u32[]{:S(2)}, u32[]{:S(2)}) collective-permute-start(bf16[3,12,11,1024]{3,1,2,0:T(8,128)(2,1)S(1)} %copy.150), channel_id=1, source_target_pairs={{1,0},{2,1},{3,2},{4,3},{5,4},{6,5},{7,6},{0,7},{9,8},{10,9},{11,1... | collective-permute-start | bytes 2433032 | tf_op jit(solution)/shard_map/ppermute | solution.py:24
  129.5 27.1 %collective-permute-start = (bf16[3,12,11,1024]{3,1,2,0:T(8,128)(2,1)S(1)}, bf16[3,12,11,1024]{3,1,2,0:T(8,128)(2,1)S(1)}, u32[]{:S(2)}, u32[]{:S(2)}) collective-permute-start(bf16[3,12,11,1024]{3,1,2,0:T(8,128)(2,1)S(1)} %copy.149), channel_id=1, source_target_pairs={{0,1},{1,2},{2,3},{3,4},{4,5},{5,6},{6,7},{7,0},{8,9},{9,10},{10,1... | collective-permute-start | bytes 2433032 | tf_op jit(solution)/shard_map/ppermute | solution.py:21
  151.6 8.1 %copy-start.4 = (bf16[3,12,11,1024]{3,2,1,0:T(8,128)(2,1)}, bf16[3,12,11,1024]{3,2,1,0:T(8,128)(2,1)S(1)}, u32[]{:S(2)}) copy-start(bf16[3,12,11,1024]{3,2,1,0:T(8,128)(2,1)S(1)} %copy.152) | copy-start | bytes 2433028
  157.1 2.5 copy-start.5
  157.2 9.0 %copy-start.2 = (bf16[3,12,12,1024]{3,2,1,0:T(8,128)(2,1)S(1)}, bf16[3,12,12,1024]{3,2,1,0:T(8,128)(2,1)}, u32[]{:S(2)}) copy-start(bf16[3,12,12,1024]{3,2,1,0:T(8,128)(2,1)} %param.29) | copy-start | bytes 2654212
  157.2 9.0 %copy-start.14 = (bf16[64,1024]{1,0:T(8,128)(2,1)S(1)}, bf16[64,1024]{1,0:T(8,128)(2,1)}, u32[]{:S(2)}) copy-start(bf16[64,1024]{1,0:T(8,128)(2,1)} %param.28) | copy-start | bytes 393220
  159.7 43.1 %collective-permute-start.3 = (bf16[3,5,34,1024]{3,2,1,0:T(8,128)(2,1)}, bf16[3,5,34,1024]{3,2,1,0:T(8,128)(2,1)}, u32[]{:S(2)}, u32[]{:S(2)}) collective-permute-start(bf16[3,5,34,1024]{3,2,1,0:T(8,128)(2,1)} %get-tuple-element.7), channel_id=1, source_target_pairs={{8,0},{16,8},{24,16},{0,24},{9,1},{17,9},{25,17},{1,25},{10,2},{18... | collective-permute-start | bytes 3133448 | tf_op jit(solution)/shard_map/ppermute | solution.py:24
  163.8 38.9 %collective-permute-start.2 = (bf16[3,5,34,1024]{3,2,1,0:T(8,128)(2,1)}, bf16[3,5,34,1024]{3,2,1,0:T(8,128)(2,1)}, u32[]{:S(2)}, u32[]{:S(2)}) collective-permute-start(bf16[3,5,34,1024]{3,2,1,0:T(8,128)(2,1)} %get-tuple-element.8), channel_id=1, source_target_pairs={{0,8},{8,16},{16,24},{24,0},{1,9},{9,17},{17,25},{25,1},{2,10},{10... | collective-permute-start | bytes 3133448 | tf_op jit(solution)/shard_map/ppermute | solution.py:21
  166.6 0.7 copy-start.6
  168.0 8.8 %collective-permute-start.4 = (bf16[3,12,11,64]{3,2,1,0:T(8,128)(2,1)}, bf16[3,12,11,64]{3,2,1,0:T(8,128)(2,1)}, u32[]{:S(2)}, u32[]{:S(2)}) collective-permute-start(bf16[3,12,11,64]{3,2,1,0:T(8,128)(2,1)} %get-tuple-element.17), channel_id=1, source_target_pairs={{0,1},{1,2},{2,3},{3,4},{4,5},{5,6},{6,7},{7,0},{8,9},{9,10},{10,1... | collective-permute-start | bytes 152072 | tf_op jit(solution)/shard_map/ppermute | solution.py:21
  169.9 7.8 %collective-permute-start.5 = (bf16[3,12,11,64]{3,2,1,0:T(8,128)(2,1)}, bf16[3,12,11,64]{3,2,1,0:T(8,128)(2,1)}, u32[]{:S(2)}, u32[]{:S(2)}) collective-permute-start(bf16[3,12,11,64]{3,2,1,0:T(8,128)(2,1)} %get-tuple-element.18), channel_id=1, source_target_pairs={{1,0},{2,1},{3,2},{4,3},{5,4},{6,5},{7,6},{0,7},{9,8},{10,9},{11,1... | collective-permute-start | bytes 152072 | tf_op jit(solution)/shard_map/ppermute | solution.py:24
  179.6 13.4 %collective-permute-start.7 = (bf16[3,5,34,64]{3,2,1,0:T(8,128)(2,1)}, bf16[3,5,34,64]{3,2,1,0:T(8,128)(2,1)}, u32[]{:S(2)}, u32[]{:S(2)}) collective-permute-start(bf16[3,5,34,64]{3,2,1,0:T(8,128)(2,1)} %get-tuple-element.15), channel_id=1, source_target_pairs={{8,0},{16,8},{24,16},{0,24},{9,1},{17,9},{25,17},{1,25},{10,2},{18... | collective-permute-start | bytes 195848 | tf_op jit(solution)/shard_map/ppermute | solution.py:24
  182.6 11.8 %collective-permute-start.6 = (bf16[3,5,34,64]{3,2,1,0:T(8,128)(2,1)}, bf16[3,5,34,64]{3,2,1,0:T(8,128)(2,1)}, u32[]{:S(2)}, u32[]{:S(2)}) collective-permute-start(bf16[3,5,34,64]{3,2,1,0:T(8,128)(2,1)} %get-tuple-element.16), channel_id=1, source_target_pairs={{0,8},{8,16},{16,24},{24,0},{1,9},{9,17},{17,25},{25,1},{2,10},{10... | collective-permute-start | bytes 195848 | tf_op jit(solution)/shard_map/ppermute | solution.py:21
  224.6 1.1 copy-start.10
  232.7 2.0 copy-start.3
  234.7 0.9 copy-start.9
  234.7 1.9 copy-start.8
  258.3 198.9 %reduce-scatter.11.cloned.1.call-start = ((), (), s32[]{:S(2)}) async-start(), calls=%async_computation.7 | async-start | bytes 270336 | tf_op jit(solution)/shard_map/reduce_scatter | solution.py:263
  261.1 315.4 %reduce-scatter.9.cloned.1.call-start = ((), (), s32[]{:S(2)}) async-start(), calls=%async_computation.6 | async-start | bytes 540672 | tf_op jit(solution)/shard_map/reduce_scatter | solution.py:260
  263.6 408.3 %reduce-scatter.13.cloned.1.call-start = ((), (), s32[]{:S(2)}) async-start(), calls=%async_computation.8 | async-start | bytes 1114112
  292.0 384.1 %copy-start.13 = (f32[3,12,12]{2,1,0:T(8,128)S(1)}, f32[3,12,12]{2,1,0:T(8,128)}, u32[]{:S(2)}) copy-start(f32[3,12,12]{2,1,0:T(8,128)} %copy.143) | copy-start | bytes 5188
  457.2 220.8 %copy-start.1 = (bf16[512,512]{1,0:T(8,128)(2,1)S(1)}, bf16[512,512]{1,0:T(8,128)(2,1)}, u32[]{:S(2)}) copy-start(bf16[512,512]{1,0:T(8,128)(2,1)} %param.22) | copy-start | bytes 1572868
Sparse Core Ops, SparseCore 0:
  258.4 81.2 reduce-scatter.6
  342.7 114.4 reduce-scatter.10
  460.0 116.4 reduce-scatter.8
  580.9 90.9 reduce-scatter.12
where the time goes:
time: 695 us; the launch traced here: 685 us
  waiting for transfers between devices  411 us (59%)
  local copies, waits for them, and re-layouts  83.9 us (12%)
  blocking collectives  79 us (11%)
  matrix products  42.7 us (6%)
  starting transfers between devices  30.1 us (4%)
  other arithmetic  22.7 us (3%)
  between operations  15.8 us (2%)
    reduce_scatter x1, waiting for transfers between devices, local(): lax.psum_scatter(grad_qkv_part.astype(jnp.bfloat16), ('lat', 'lon'), scat...  118 us
    reduce_scatter x1, waiting for transfers between devices, local(): lax.psum_scatter(grad_proj_part.astype(jnp.bfloat16), ('lat', 'lon'), sca...  117 us
    unnamed x5, waiting for transfers between devices  94.2 us
    all_gather x1, blocking collectives, local(): column_rows = lax.all_gather(latent_band, 'enc', axis=1, tiled=True)  53.1 us
    reduce_scatter x1, waiting for transfers between devices, local(): lax.psum_scatter(sums_wide.astype(jnp.bfloat16), 'enc', scatter_dimension...  47.7 us
    unnamed x39, local copies, waits for them, and re-layouts  40.9 us
    ppermute x4, waiting for transfers between devices, padded(): lax.ppermute(lax.slice_in_dim(block, 0, width, axis=dim), axis, backward)  26.1 us
    all_to_all x1, blocking collectives, local(): lax.all_to_all(column_rows, 'lat', split_axis=1, concat_axis=2, tiled=True)  25.9 us
  transfers between devices with their start and end apart: 12, of which 10 were waited for; matrix products, arithmetic and copies ran while one was open for 7% of the time, Pallas kernels for 0%

commit v1 on v0

v1 whole, which is shorter than its diff:
```python
import functools

import jax
import jax.numpy as jnp
import numpy as np
from jax import lax
from jax.experimental import pallas as pl
from jax.experimental.pallas import tpu as pltpu
from jax.sharding import PartitionSpec as P

PHEADS = 16
WIN_LAT = 6
WIN_LON = 12
HD = 64
LEVELS = 3
MESH = pl.DeviceIdType.MESH

epsilon = 1e-05
F32 = jnp.float32
BF16 = jnp.bfloat16


def layer_norm(values):
    centre = jnp.mean(values, axis=-1, keepdims=True)
    centred = values - centre
    variance = jnp.mean(centred * centred, axis=-1, keepdims=True)
    inverse = lax.rsqrt(variance + epsilon)
    return (centred * inverse, inverse)


def encode(
    atmos,
    land_sea,
    level_count,
    atm_weight,
    land_weight,
    level_embed,
    latent_query,
    key_weight,
    value_weight,
):
    row_count, col_count, levels, pixels = atmos.shape
    patches = row_count * col_count
    embedded = jnp.dot(
        atmos.reshape(patches * levels, pixels), atm_weight, preferred_element_type=jnp.float32
    )
    embedded = embedded.reshape(patches, levels, -1)
    static = jnp.dot(
        land_sea.reshape(patches, -1).astype(jnp.bfloat16),
        land_weight,
        preferred_element_type=jnp.float32,
    )
    embedded = embedded + level_embed[None, :, :] + static[:, None, :]
    normed, unused_scale = layer_norm(embedded)
    tokens = normed.astype(jnp.bfloat16).reshape(patches * levels, -1)
    key_rows = jnp.dot(tokens, key_weight, preferred_element_type=jnp.float32).astype(jnp.bfloat16)
    value_rows = jnp.dot(tokens, value_weight, preferred_element_type=jnp.float32).astype(
        jnp.bfloat16
    )
    key_rows = key_rows.reshape(patches, levels, PHEADS, -1)
    value_rows = value_rows.reshape(patches, levels, PHEADS, -1)
    queries = latent_query.reshape(latent_query.shape[0], PHEADS, -1)
    score_scale = key_rows.shape[-1] ** (-0.5)
    scores = (
        jnp.einsum("mhc,plhc->phml", queries, key_rows, preferred_element_type=jnp.float32)
        * score_scale
    )
    present = jnp.arange(levels, dtype=jnp.int32)[None, :] < level_count.reshape(patches, 1)
    weights = jnp.where(present[:, None, None, :], jnp.exp(scores), 0.0)
    level_probs = (weights / jnp.sum(weights, axis=-1, keepdims=True)).astype(jnp.bfloat16)
    attended = jnp.einsum(
        "phml,plhc->pmhc", level_probs, value_rows, preferred_element_type=jnp.float32
    )
    attended = attended.astype(jnp.bfloat16).reshape(row_count, col_count, queries.shape[0], -1)
    return attended.transpose(2, 0, 1, 3)


def merge_patches(fine, merge_weight):
    levels, row_count, col_count, width = fine.shape
    grouped = fine.reshape(levels, row_count // 2, 2, col_count // 2, 2, width).transpose(
        0, 1, 3, 4, 2, 5
    )
    grouped = grouped.reshape(levels, row_count // 2, col_count // 2, 4 * width)
    merge_in = layer_norm(grouped.astype(jnp.float32))[0].astype(jnp.bfloat16)
    merged = jnp.dot(
        merge_in.reshape(-1, 4 * width), merge_weight, preferred_element_type=jnp.float32
    ).astype(jnp.bfloat16)
    return merged.reshape(levels, row_count // 2, col_count // 2, -1)


class Sizes:
    def __init__(self, enc, lat, lon, band, block, width):
        self.enc, self.lat, self.lon = enc, lat, lon
        self.band, self.block, self.width = band, block, width
        self.share = enc // lat
        self.rows, self.cols = self.share * band, lat * block
        self.slots = self.share * lat
        self.block_tokens = LEVELS * band * block
        self.block_rows = -(-self.block_tokens // 16) * 16
        self.row_tokens = LEVELS * self.cols
        self.tokens = self.rows * self.row_tokens
        self.half = self.tokens // 2
        self.packed = -(-self.half // 16) * 16
        self.group = lat * lon
        self.chunk = width // self.group
        self.total_rows = self.rows * lat


def block_order(size):
    matrix = np.zeros((size.tokens, size.slots * size.block_rows), np.float32)
    for a in range(size.rows):
        for level in range(LEVELS):
            for b in range(size.cols):
                slot = (a // size.band) * size.lat + b // size.block
                inner = (level * size.band + a % size.band) * size.block + b % size.block
                token = a * size.row_tokens + level * size.cols + b
                matrix[token, slot * size.block_rows + inner] = 1.0
    return matrix


def token_place(size, token):
    row = ((token.astype(F32) + 0.5) * (1.0 / size.row_tokens)).astype(jnp.int32)
    rest = token - row * size.row_tokens
    level = ((rest.astype(F32) + 0.5) * (1.0 / size.cols)).astype(jnp.int32)
    return row, level, rest - level * size.cols


def dot(a, b):
    return jnp.dot(a, b, preferred_element_type=F32)


def dot_tb(a, b):
    return lax.dot_general(a, b, (((1,), (1,)), ((), ())), preferred_element_type=F32)


def dot_ta(a, b):
    return lax.dot_general(a, b, (((0,), (0,)), ((), ())), preferred_element_type=F32)


def pack_pair(values, odd, half):
    top, bottom = values[:half], values[half:]
    left = lax.broadcasted_iota(jnp.int32, top.shape, 1) < HD
    if odd:
        return jnp.where(left, pltpu.roll(top, HD, 1), bottom)
    return jnp.where(left, top, pltpu.roll(bottom, HD, 1))


def layer_kernel(
    size,
    factor,
    lat_shift,
    lon_shift,
    x_ref,
    order_ref,
    wqkv_ref,
    proj_ref,
    cot_ref,
    latent_out,
    weight_out,
    lat_buf,
    normed_ref,
    inv_ref,
    hid_ref,
    halo_f,
    halo,
    halo_left,
    halo_up,
    halo_diag,
    back_f,
    back,
    back_right,
    back_down,
    back_diag,
    msg,
    msg_in,
    grad,
    grad_in,
    multi_send,
    multi_recv,
    halo_send,
    halo_recv,
    back_send,
    back_recv,
    msg_send,
    msg_recv,
    grad_send,
    grad_recv,
):
    enc, lat, lon = lax.axis_index("enc"), lax.axis_index("lat"), lax.axis_index("lon")
    n_enc, n_lat, n_lon, group = size.enc, size.lat, size.lon, size.group
    home = enc // size.share
    tokens, half, packed = size.tokens, size.half, size.packed
    away = home != lat

    barrier = pltpu.get_barrier_semaphore()

    def greet(*device):
        pl.semaphore_signal(barrier, inc=1, device_id=device, device_id_type=MESH)

    def greet_heads(k, carry):
        greet((enc + k) % n_enc, lat, lon)
        return carry

    lax.fori_loop(1, n_enc, greet_heads, 0)
    member = lat * n_lon + lon

    def greet_tiles(k, carry):
        other = (member + k) % group
        greet(enc, other // n_lon, other % n_lon)
        return carry

    lax.fori_loop(1, group, greet_tiles, 0)

    def greet_targets(k, carry):
        greet(k, home, lon)
        return carry

    @pl.when(away)
    def _():
        lax.fori_loop(0, n_enc, greet_targets, 0)

    def greet_sources(k, carry):
        source = lat * size.share + k // (n_lat - 1)
        greet(source, (lat + 1 + k % (n_lat - 1)) % n_lat, lon)
        return carry

    lax.fori_loop(0, size.share * (n_lat - 1), greet_sources, 0)
    expected = n_enc - 1 + group - 1 + size.share * (n_lat - 1)
    pl.semaphore_wait(barrier, jnp.where(away, expected + n_enc, expected))

    slot = (enc % size.share) * n_lat + lat

    def multicast(k, place):
        return pltpu.make_async_remote_copy(
            src_ref=x_ref,
            dst_ref=lat_buf.at[place],
            send_sem=multi_send.at[k],
            recv_sem=multi_recv.at[place],
            device_id=((enc + k) % n_enc, home, lon),
            device_id_type=MESH,
        )

    own_block = pltpu.make_async_copy(x_ref, lat_buf.at[slot], multi_recv.at[slot])

    @pl.when(away)
    def _():
        multicast(0, slot).start()

    @pl.when(jnp.logical_not(away))
    def _():
        own_block.start()

    def send_block(k, carry):
        multicast(k, slot).start()
        return carry

    lax.fori_loop(1, n_enc, send_block, 0)

    halo_f[:, 3 * HD :] = dot_tb(cot_ref[...], proj_ref[...])
    row_shift, col_shift = lat_shift[0], lon_shift[0]

    def rolled_source(token):
        row, level, col = token_place(size, token)
        row, col = row - row_shift, col - col_shift
        row = jnp.where(row < 0, row + size.rows, row)
        col = jnp.where(col < 0, col + size.cols, col)
        return row * size.row_tokens + level * size.cols + col

    square = (tokens, tokens)
    roll_from = rolled_source(lax.broadcasted_iota(jnp.int32, (tokens, 1), 0))
    roll_matrix = jnp.where(
        roll_from == lax.broadcasted_iota(jnp.int32, square, 1), 1.0, 0.0
    ).astype(BF16)
    roll_to = rolled_source(lax.broadcasted_iota(jnp.int32, (1, tokens), 1))
    unroll_matrix = jnp.where(
        roll_to == lax.broadcasted_iota(jnp.int32, square, 0), 1.0, 0.0
    ).astype(BF16)
    row_of, unused, col_of = token_place(size, lax.broadcasted_iota(jnp.int32, (tokens, 1), 0))

    def arrive(k, carry):
        local_slot = jnp.logical_and(k == slot, jnp.logical_not(away))

        @pl.when(local_slot)
        def _():
            own_block.wait()

        @pl.when(jnp.logical_not(local_slot))
        def _():
            multicast(0, k).wait_recv()

        return carry

    lax.fori_loop(0, size.slots, arrive, 0)

    step_rows = tokens // 3
    blocks = lat_buf[...].reshape(size.slots * size.block_rows, size.width)

    def normalise(k, carry):
        rows = pl.ds(pl.multiple_of(k * step_rows, 16), step_rows)
        values = dot(order_ref[rows, :], blocks)
        normed, inverse = layer_norm(values)
        normed_ref[rows, :] = normed
        inv_ref[rows, :] = jnp.broadcast_to(inverse, (step_rows, 128))
        hidden = normed.astype(BF16)
        hid_ref[rows, :] = hidden
        halo_f[rows, : 3 * HD] = dot(hidden, wqkv_ref[...])
        return carry

    lax.fori_loop(0, 3, normalise, 0)
    halo[...] = halo_f[...].astype(BF16)

    next_lat, last_lat = (lat + 1) % n_lat, (lat + n_lat - 1) % n_lat
    next_lon, last_lon = (lon + 1) % n_lon, (lon + n_lon - 1) % n_lon
    upper = tokens - packed

    def exchange(source, target, send, recv, k, *place):
        return pltpu.make_async_remote_copy(
            src_ref=source,
            dst_ref=target,
            send_sem=send.at[k],
            recv_sem=recv.at[k],
            device_id=(enc, *place),
            device_id_type=MESH,
        )

    lower_rows = halo.at[pl.ds(upper, packed)]
    halo_copies = [
        exchange(halo, halo_left, halo_send, halo_recv, 0, lat, next_lon),
        exchange(lower_rows, halo_diag, halo_send, halo_recv, 1, next_lat, next_lon),
        exchange(lower_rows, halo_up, halo_send, halo_recv, 2, next_lat, lon),
    ]
    for copy in halo_copies:
        copy.start()
    for copy in halo_copies:
        copy.wait_recv()

    own_row = row_of < size.rows - row_shift
    own_col = col_of < size.cols - col_shift
    near = jnp.where(own_col, halo[...].astype(F32), halo_left[...].astype(F32))
    far = jnp.where(own_col[upper:], halo_up[...].astype(F32), halo_diag[...].astype(F32))
    spread = jnp.concatenate([near[:upper], jnp.where(own_row[upper:], near[upper:], far)], axis=0)
    rolled = dot(roll_matrix, spread.astype(BF16))

    win = size.half
    score_scale = HD ** (-0.5)
    window_rows = WIN_LAT * size.row_tokens
    for w in range(tokens // window_rows):
        part = rolled[w * win : (w + 1) * win].astype(BF16)
        queries, keys = part[:, :HD], part[:, HD : 2 * HD]
        values, grads = part[:, 2 * HD : 3 * HD], part[:, 3 * HD :]
        first = lat * size.rows + w * WIN_LAT
        row_a = token_place(size, lax.broadcasted_iota(jnp.int32, (win, 1), 0))[0]
        row_b = token_place(size, lax.broadcasted_iota(jnp.int32, (1, win), 1))[0]
        side_a = jnp.where(row_a + first < row_shift, 1, 0)
        side_b = jnp.where(row_b + first < row_shift, 1, 0)
        scores = dot_tb(queries, keys) * score_scale
        weights = jnp.where(side_a == side_b, jnp.exp(scores), 0.0)
        probs = weights / jnp.sum(weights, axis=-1, keepdims=True)
        low = probs.astype(BF16)
        grad_probs = dot_tb(grads, values)
        grad_scores = probs * (
            grad_probs - jnp.sum(grad_probs * probs, axis=-1, keepdims=True)
        )
        grad_low = grad_scores.astype(BF16)
        there = pl.ds(w * win, win)
        back_f[there, :HD] = dot(grad_low, keys) * score_scale
        back_f[there, HD : 2 * HD] = dot_ta(grad_low, queries) * score_scale
        back_f[there, 2 * HD : 3 * HD] = dot_ta(low, grads)
        back_f[there, 3 * HD :] = dot(low, values)
    back[...] = back_f[...].astype(BF16)

    upper_rows = back.at[pl.ds(0, packed)]
    back_copies = [
        exchange(back, back_right, back_send, back_recv, 0, lat, last_lon),
        exchange(upper_rows, back_diag, back_send, back_recv, 1, last_lat, last_lon),
        exchange(upper_rows, back_down, back_send, back_recv, 2, last_lat, lon),
    ]
    for copy in back_copies:
        copy.start()
    for copy in back_copies:
        copy.wait_recv()

    own_row = row_of >= row_shift
    own_col = col_of >= col_shift
    near = jnp.where(own_col, back[...].astype(F32), back_right[...].astype(F32))
    far = jnp.where(own_col[:packed], back_down[...].astype(F32), back_diag[...].astype(F32))
    spread = jnp.concatenate(
        [jnp.where(own_row[:packed], near[:packed], far), near[packed:]], axis=0
    )
    own = dot(unroll_matrix, spread.astype(BF16)).astype(BF16)
    grad_rows, heads_out = own[:, : 3 * HD], own[:, 3 * HD :]

    head_part = dot_tb(grad_rows, wqkv_ref[...])
    ones = jnp.ones((8, size.width), BF16)
    sums = dot_tb(ones, head_part.astype(BF16))
    cross = dot_tb(ones, (head_part * normed_ref[...]).astype(BF16))
    lanes = 4 * 128
    pad = jnp.zeros((8, lanes - tokens), F32)
    sums = jnp.concatenate([sums, pad], axis=1)
    cross = jnp.concatenate([cross, pad], axis=1)
    index = lax.broadcasted_iota(jnp.int32, (8, 128), 0)
    extra = jnp.zeros((8, 128), F32)
    for k in range(4):
        columns = slice(k * 128, (k + 1) * 128)
        extra = jnp.where(index == k, sums[:, columns], extra)
        extra = jnp.where(index == k + 4, cross[:, columns], extra)
    for pair in range(n_enc // 2):
        values = head_part[:, pair * 128 : (pair + 1) * 128]
        for odd in range(2):
            message = pack_pair(values, odd, half)
            msg[2 * pair + odd] = jnp.concatenate([message, extra], axis=0).astype(BF16)

    def head_copy(k, target):
        return pltpu.make_async_remote_copy(
            src_ref=msg.at[target],
            dst_ref=msg_in.at[k],
            send_sem=msg_send.at[k],
            recv_sem=msg_recv.at[k],
            device_id=(target, lat, lon),
            device_id_type=MESH,
        )

    def send_head(k, carry):
        head_copy(k, (enc + k) % n_enc).start()
        return carry

    lax.fori_loop(1, n_enc, send_head, 0)

    grad[:, :, : 3 * HD] = (
        (dot_ta(hid_ref[...], grad_rows) * factor)
        .astype(BF16)
        .reshape(group, size.chunk, 3 * HD)
    )
    grad[:, :, 3 * HD :] = (
        (dot_ta(cot_ref[...], heads_out) * factor).astype(BF16).reshape(group, size.chunk, HD)
    )

    def grad_copy(k, target):
        return pltpu.make_async_remote_copy(
            src_ref=grad.at[target],
            dst_ref=grad_in.at[k],
            send_sem=grad_send.at[k],
            recv_sem=grad_recv.at[k],
            device_id=(enc, target // n_lon, target % n_lon),
            device_id_type=MESH,
        )

    def send_grad(k, carry):
        grad_copy(k, (member + k) % group).start()
        return carry

    lax.fori_loop(1, group, send_grad, 0)

    columns = pl.ds(pl.multiple_of((enc // 2) * 128, 128), 128)
    odd = enc % 2 == 1

    def own_share(values):
        return jnp.where(odd, pack_pair(values, 1, half), pack_pair(values, 0, half))

    def side_by_side(column):
        left = lax.broadcasted_iota(jnp.int32, (half, 128), 1) < HD
        return jnp.where(left, column[:half], column[half:])

    normed_own = own_share(normed_ref[:, columns])
    cot_own = own_share(cot_ref[:, columns].astype(F32))
    inverse_own = side_by_side(inv_ref[...])

    def take_head(k, total):
        head_copy(k, enc).wait_recv()
        return total + msg_in[k].astype(F32)

    total = lax.fori_loop(1, n_enc, take_head, msg[enc].astype(F32))
    token = lax.broadcasted_iota(jnp.int32, (tokens, 1), 0)
    place = lax.broadcasted_iota(jnp.int32, (tokens, 128), 1)
    line = jnp.right_shift(token, 7)
    pick = jnp.where(token - line * 128 == place, 1.0, 0.0)
    means = lax.dot_general(
        pick,
        total[half:packed],
        (((1,), (1,)), ((), ())),
        precision=lax.Precision.HIGHEST,
        preferred_element_type=F32,
    ) * (1.0 / size.width)
    which = lax.broadcasted_iota(jnp.int32, (tokens, 8), 1)
    mean_grad = jnp.sum(jnp.where(which == line, means, 0.0), axis=-1, keepdims=True)
    mean_cross = jnp.sum(jnp.where(which == line + 4, means, 0.0), axis=-1, keepdims=True)
    latent_out[...] = (
        cot_own
        + inverse_own
        * (total[:half] - side_by_side(mean_grad) - normed_own * side_by_side(mean_cross))
    ).astype(BF16)

    def take_grad(k, total):
        grad_copy(k, member).wait_recv()
        return total + grad_in[k].astype(F32)

    weight_out[...] = lax.fori_loop(1, group, take_grad, grad[member].astype(F32))

    @pl.when(away)
    def _():
        multicast(0, slot).wait_send()

    def sent_block(k, carry):
        multicast(k, slot).wait_send()
        return carry

    lax.fori_loop(1, n_enc, sent_block, 0)
    for copy in halo_copies + back_copies:
        copy.wait_send()

    def sent_head(k, carry):
        head_copy(k, (enc + k) % n_enc).wait_send()
        return carry

    lax.fori_loop(1, n_enc, sent_head, 0)

    def sent_grad(k, carry):
        grad_copy(k, (member + k) % group).wait_send()
        return carry

    lax.fori_loop(1, group, sent_grad, 0)


def layer(size, lat_shift, lon_shift, block, wqkv, proj, cot):
    tokens, packed = size.tokens, size.packed
    vmem = pl.BlockSpec(memory_space=pltpu.VMEM)
    smem = pl.BlockSpec(memory_space=pltpu.SMEM)
    factor = (tokens * size.group) ** (-0.5)
    wide = 4 * HD
    dma = pltpu.SemaphoreType.DMA
    return pl.pallas_call(
        functools.partial(layer_kernel, size, factor),
        out_shape=(
            jax.ShapeDtypeStruct((size.half, 128), BF16),
            jax.ShapeDtypeStruct((size.chunk, wide), F32),
        ),
        in_specs=[smem, smem] + [vmem] * 5,
        out_specs=(vmem, vmem),
        scratch_shapes=[
            pltpu.VMEM((size.slots, size.block_rows, size.width), BF16),
            pltpu.VMEM((tokens, size.width), F32),
            pltpu.VMEM((tokens, 128), F32),
            pltpu.VMEM((tokens, size.width), BF16),
            pltpu.VMEM((tokens, wide), F32),
            pltpu.VMEM((tokens, wide), BF16),
            pltpu.VMEM((tokens, wide), BF16),
            pltpu.VMEM((packed, wide), BF16),
            pltpu.VMEM((packed, wide), BF16),
            pltpu.VMEM((tokens, wide), F32),
            pltpu.VMEM((tokens, wide), BF16),
            pltpu.VMEM((tokens, wide), BF16),
            pltpu.VMEM((packed, wide), BF16),
            pltpu.VMEM((packed, wide), BF16),
            pltpu.VMEM((size.enc, packed, 128), BF16),
            pltpu.VMEM((size.enc, packed, 128), BF16),
            pltpu.VMEM((size.group, size.chunk, wide), BF16),
            pltpu.VMEM((size.group, size.chunk, wide), BF16),
            dma((size.enc,)),
            dma((size.slots,)),
            dma((3,)),
            dma((3,)),
            dma((3,)),
            dma((3,)),
            dma((size.enc,)),
            dma((size.enc,)),
            dma((size.group,)),
            dma((size.group,)),
        ],
        compiler_params=pltpu.CompilerParams(
            collective_id=0, has_side_effects=True, vmem_limit_bytes=56 * 1024 * 1024
        ),
    )(lat_shift, lon_shift, block, jnp.asarray(block_order(size), BF16), wqkv, proj, cot)


def layer_part(size, latent_band, lat_shift, lon_shift, qkv_weight, proj_weight, cotangent):
    block = latent_band.reshape(size.block_tokens, size.width)
    block = jnp.pad(block, ((0, size.block_rows - size.block_tokens), (0, 0)))
    cot = cotangent.transpose(1, 0, 2, 3).reshape(size.tokens, size.width)
    packed_latent, weights = layer(
        size, lat_shift, lon_shift, block, qkv_weight, proj_weight, cot
    )
    latent = packed_latent.reshape(size.half, 2, HD).transpose(1, 0, 2)
    latent = latent.reshape(size.rows, LEVELS, size.cols, HD).transpose(1, 0, 2, 3)
    return latent, weights[:, : 3 * HD], weights[:, 3 * HD :].T


def local(
    atmos,
    land_sea,
    level_count,
    atm_weight,
    land_weight,
    level_embed,
    latent_query,
    key_weight,
    value_weight,
    merge_weight,
    lat_shift,
    lon_shift,
    qkv_weight,
    proj_weight,
    cotangent,
):
    fine_band = encode(
        atmos,
        land_sea,
        level_count,
        atm_weight,
        land_weight,
        level_embed,
        latent_query,
        key_weight,
        value_weight,
    )
    latent_band = merge_patches(fine_band, merge_weight)
    unused, band, block, width = latent_band.shape
    size = Sizes(
        lax.axis_size("enc"), lax.axis_size("lat"), lax.axis_size("lon"), band, block, width
    )
    return layer_part(
        size, latent_band, lat_shift, lon_shift, qkv_weight, proj_weight, cotangent
    )


def solution(mesh):
    return jax.shard_map(
        local,
        mesh=mesh,
        in_specs=(
            P("enc", ("lon", "lat"), None, None),
            P("enc", ("lon", "lat"), None),
            P("enc", ("lon", "lat")),
            P(),
            P(),
            P(),
            P(),
            P(),
            P(),
            P(),
            P(),
            P(),
            P(None, "enc"),
            P("enc", None),
            P(None, "lat", "lon", None),
        ),
        out_specs=(
            P(None, "lat", "lon", "enc"),
            P(("lat", "lon"), "enc"),
            P("enc", ("lat", "lon")),
        ),
        check_vma=False,
    )
```

time: 695 us -> 128 us (0.18); the launches traced: 685 us -> 127 us
  waiting for transfers between devices: 411 us -> 0 us
  Pallas kernels: 0 us -> 101 us
  blocking collectives: 79 us -> 0 us
  local copies, waits for them, and re-layouts: 83.9 us -> 12.3 us
  matrix products: 42.7 us -> 9.95 us
  starting transfers between devices: 30.1 us -> 0 us
  other arithmetic: 22.7 us -> 1.93 us
  between operations: 15.8 us -> 2.18 us
    reduce_scatter x3 -> x0, waiting for transfers between devices: 282 us -> none  [the longest x1 118 us: local(): lax.psum_scatter(grad_qkv_part.astype(jnp.bfloat16), ('lat', 'lon'), scat...]
    pallas_call x0 -> x1, Pallas kernels: none -> 101 us  [layer(): pl.pallas_call(functools.partial(layer_kernel, size, factor), out_shape=(...]
    unnamed x5 -> x0, waiting for transfers between devices: 94.2 us -> none
    all_gather x1 -> x0, blocking collectives: 53.1 us -> none  [local(): column_rows = lax.all_gather(latent_band, 'enc', axis=1, tiled=True)]
    unnamed x39 -> x15, local copies, waits for them, and re-layouts: 40.9 us -> 3.08 us
    ppermute x8 -> x0, waiting for transfers between devices: 34 us -> none  [the longest x4 26.1 us: padded(): lax.ppermute(lax.slice_in_dim(block, 0, width, axis=dim), axis, backward)]
    ppermute x8 -> x0, starting transfers between devices: 30 us -> none  [the longest x4 20.5 us: padded(): lax.ppermute(lax.slice_in_dim(block, 0, width, axis=dim), axis, backward)]
    dot_general x11 -> x0, matrix products: 28.7 us -> none  [the longest x1 9.12 us: local(): jnp.dot(hidden_region, qkv_weight, preferred_element_type=jnp.float32)]
  transfers between devices with their start and end apart: 12 -> 0, of which waited for: 10 -> 0; matrix products, arithmetic and copies ran while one was open for 7% -> 0% of each run, Pallas kernels for 0% -> 0%
where the time goes in v1:
time: 128 us; the launch traced here: 127 us
  Pallas kernels  101 us (79%)
  local copies, waits for them, and re-layouts  12.3 us (10%)
  matrix products  9.95 us (8%)
  between operations  2.18 us (2%)
  other arithmetic  1.93 us (2%)
    pallas_call x1, Pallas kernels, layer(): pl.pallas_call(functools.partial(layer_kernel, size, factor), out_shape=(...  101 us
    dot_general x1, matrix products, merge_patches(): jnp.dot(merge_in.reshape(-1, 4 * width), merge_weight, preferred_element_...  3.15 us
    unnamed x15, local copies, waits for them, and re-layouts  3.08 us

profile of v1, /device:TPU:1, one launch (start us, length us, event | category | flops | bytes accessed | tf_op | source)
XLA Modules:
  0.0 127.2 jit_solution(2311936066241168544)
XLA Ops:
  0.6 0.8 convert_element_type.56
  1.5 1.0 fusion.34
  2.5 1.8 %fusion.32 = (f32[36,13]{0,1:T(8,128)S(1)}, f32[36,13,512]{2,0,1:T(8,128)S(1)}) fusion(f32[36,512]{1,0:T(8,128)S(1)} %fusion.34, f32[13,512]{1,0:T(8,128)} %param.21, bf16[500,512]{1,0:T(8,128)(2,1)} %param.19, bf16[36,13,500]{2,1,0:T(8,128)(2,1)} %bitcast.46), kind=kOutput, calls=%fused_computation.34 | convolution fusion | flops 240334384 | bytes 2040688 | tf_op jit(solution)/shard_map/dot_general | solution.py:44
  4.3 0.3 multiply_reduce_fusion
  4.6 0.2 multiply_convert_fusion
  4.9 0.2 copy.28
  5.0 0.2 reshape.107
  5.2 0.4 convolution_convert_fusion
  5.7 1.0 reshape.109
  6.7 0.1 reshape.110
  6.9 2.4 %fusion.33 = (f32[36,16,3]{0,2,1:T(4,128)S(1)}, f32[36,16,3,13]{0,2,3,1:T(4,128)S(1)}) fusion(bf16[3,16,32,1]{2,1,0,3:T(8,128)(2,1)S(1)} %bitcast.45, bf16[36,13,16,32]{3,2,1,0:T(8,128)(2,1)S(1)} %reshape.109, pred[36,13]{0,1:T(8,128)(4,1)S(1)} %iota_compare_fusion), kind=kOutput, calls=%fused_computation.35 | convolution fusion | flops 1503360 | bytes 579540 | tf_op jit(solution)/shard_map/mhc,plhc->phml/dot_general | solution.py:65
  9.4 1.3 %copy.32 = bf16[36,16,3,13]{3,2,1,0:T(4,128)(2,1)S(1)} copy(bf16[36,16,3,13]{0,2,3,1:T(4,128)(2,1)S(1)} %divide_convert_fusion) | data formatting | bytes 89856 | tf_op jit(solution)/shard_map/convert_element_type | solution.py:70
  10.7 0.4 convolution_convert_fusion.1
  11.1 1.1 reshape.108
  12.2 0.7 fusion.11
  13.0 0.3 reshape.119
  13.3 0.1 reshape.117
  13.5 0.2 fusion.31
  13.7 0.3 multiply_reduce_fusion.1
  14.0 0.1 rsqrt.21
  14.2 0.1 copy.76
  14.3 0.2 reshape.115
  14.5 3.2 %convolution_convert_fusion.2 = bf16[27,1024]{1,0:T(8,128)(2,1)S(1)} fusion(bf16[2048,1024]{1,0:T(8,128)(2,1)} %param.25, f32[27,2048]{1,0:T(8,128)S(1)} %reshape.115, f32[27]{0:T(128)S(1)} %rsqrt.21, f32[27]{0:T(128)S(1)} %div.27), kind=kOutput, calls=%fused_computation.15 | convolution fusion | flops 113439744 | bytes 4471000 | tf_op jit(solution)/shard_map/dot_general | solution.py:85
  17.7 0.6 pad.4.x_ref
  18.4 1.1 reshape.112.cot_ref
  19.6 1.0 copy.36.wqkv_ref
  21.8 100.8 %shard_map.175 = (bf16[216,128]{1,0:T(8,128)(2,1)}, f32[32,256]{1,0:T(8,128)}) custom-call(s32[1]{0:T(128)S(6)} %copy.78.lat_shift, s32[1]{0:T(128)S(6)} %copy.79.lon_shift, bf16[32,1024]{1,0:T(8,128)(2,1)} %pad.4.x_ref, bf16[432,512]{1,0:T(8,128)(2,1)} %constant.20.clone.order_ref, bf16[1024,192]{1,0:T(8,128)(2,1)} %copy.36.wqkv_ref, ...), custom_call_target="tpu_custom_call" | custom-call | tf_op jit(solution)/shard_map/pallas_call | solution.py:531
  122.7 0.9 copy.37
  123.6 0.1 copy.38
  123.8 0.7 copy.39
  124.4 1.4 %slice_bitcast_fusion = f32[64,32]{0,1:T(8,128)} fusion(f32[32,256]{1,0:T(8,128)} %get-tuple-element.6), kind=kLoop, calls=%fused_computation.27 | loop fusion | bytes 16384 | tf_op jit(solution)/shard_map/transpose | solution.py:584
  125.8 1.4 %copy.80 = f32[32,192]{1,0:T(8,128)} copy(f32[32,192]{1,0:T(8,128)} %bitcast.44) | data formatting | bytes 49152
  (24 shorter events, 0.5 us)
Async XLA Ops:
  0.6 4.6 %copy-start = (bf16[512,512]{1,0:T(8,128)(2,1)S(1)}, bf16[512,512]{1,0:T(8,128)(2,1)}, u32[]{:S(2)}) copy-start(bf16[512,512]{1,0:T(8,128)(2,1)} %param.23) | copy-start | bytes 1572868
  5.6 1.1 copy-start.5
  5.6 1.2 copy-start.4
  9.3 1.4 %copy-start.2 = (bf16[512,512]{1,0:T(8,128)(2,1)S(1)}, bf16[512,512]{1,0:T(8,128)(2,1)}, u32[]{:S(2)}) copy-start(bf16[512,512]{1,0:T(8,128)(2,1)} %param.24) | copy-start | bytes 1572868
  14.5 3.8 %copy-start.1 = (bf16[3,12,12,1024]{3,2,1,0:T(8,128)(2,1)S(1)}, bf16[3,12,12,1024]{3,2,1,0:T(8,128)(2,1)}, u32[]{:S(2)}) copy-start(bf16[3,12,12,1024]{3,2,1,0:T(8,128)(2,1)} %param.30) | copy-start | bytes 2654212
  18.4 1.1 copy-start.3

commit v2 on v1

--- a/solution.py
+++ b/solution.py
@@ -156,7 +156,8 @@
     proj_ref,
     cot_ref,
     latent_out,
-    weight_out,
+    qkv_out,
+    proj_out,
     lat_buf,
     normed_ref,
     inv_ref,
@@ -166,16 +167,25 @@
     halo_left,
     halo_up,
     halo_diag,
+    halo_right,
     back_f,
     back,
     back_right,
     back_down,
     back_diag,
+    back_left,
     msg,
     msg_in,
+    part_out,
+    part_in,
     grad,
     grad_in,
-    multi_send,
+    mid,
+    mid_in,
+    total_out,
+    total_in,
+    own_send,
+    far_send,
     multi_recv,
     halo_send,
     halo_recv,
@@ -183,8 +193,12 @@
     back_recv,
     msg_send,
     msg_recv,
+    part_send,
+    part_recv,
     grad_send,
     grad_recv,
+    total_send,
+    total_recv,
 ):
     enc, lat, lon = lax.axis_index("enc"), lax.axis_index("lat"), lax.axis_index("lon")
     n_enc, n_lat, n_lon, group = size.enc, size.lat, size.lon, size.group
@@ -228,69 +242,127 @@
     expected = n_enc - 1 + group - 1 + size.share * (n_lat - 1)
     pl.semaphore_wait(barrier, jnp.where(away, expected + n_enc, expected))
 
-    slot = (enc % size.share) * n_lat + lat
-
-    def multicast(k, place):
+    share = size.share
+    place = enc % share
+    slot = place * n_lat + lat
+    order = (0, 1, 3, 2) if share == 4 else tuple(range(share))
+    sides = (1, n_lat - 1) if n_lat > 2 else (1,)
+    relay = jnp.logical_not(away)
+    if n_lat == 4:
+        passes_on = home == (lat + jnp.where(lat % 2 == 0, n_lat - 1, 1)) % n_lat
+    else:
+        passes_on = None
+    opposite = (lat + 2) % n_lat
+
+    def block_copy(source, k, send, target):
         return pltpu.make_async_remote_copy(
-            src_ref=x_ref,
-            dst_ref=lat_buf.at[place],
-            send_sem=multi_send.at[k],
-            recv_sem=multi_recv.at[place],
-            device_id=((enc + k) % n_enc, home, lon),
+            src_ref=source,
+            dst_ref=lat_buf.at[k],
+            send_sem=send,
+            recv_sem=multi_recv.at[k],
+            device_id=target,
             device_id_type=MESH,
         )
 
     own_block = pltpu.make_async_copy(x_ref, lat_buf.at[slot], multi_recv.at[slot])
 
+    def first_copy(step):
+        target = (home * share + (place + step) % share, home, lon)
+        return block_copy(x_ref, slot, own_send.at[step], target)
+
+    def pass_copy(k, index, group):
+        return block_copy(lat_buf.at[k], k, far_send.at[index], (group * share + place, lat, lon))
+
+    @pl.when(relay)
+    def _():
+        own_block.start()
+
     @pl.when(away)
     def _():
-        multicast(0, slot).start()
-
-    @pl.when(jnp.logical_not(away))
-    def _():
-        own_block.start()
-
-    def send_block(k, carry):
-        multicast(k, slot).start()
-        return carry
-
-    lax.fori_loop(1, n_enc, send_block, 0)
+        first_copy(0).start()
+
+    for step in order[1:]:
+        first_copy(step).start()
 
     halo_f[:, 3 * HD :] = dot_tb(cot_ref[...], proj_ref[...])
     row_shift, col_shift = lat_shift[0], lon_shift[0]
-
-    def rolled_source(token):
-        row, level, col = token_place(size, token)
+    win = size.half
+    win_pad = size.packed
+
+    def number(rows, start=0):
+        return start + lax.broadcasted_iota(jnp.int32, (rows, 1), 0)
+
+    def column_of(rows, start=0):
+        return token_place(size, number(rows, start))[2]
+
+    def one_hot(index, columns):
+        lane = lax.broadcasted_iota(jnp.int32, (index.shape[0], columns), 1)
+        return jnp.where(index == lane, 1.0, 0.0).astype(BF16)
+
+    low_rows = -(-(WIN_LAT - 1) * size.row_tokens // 16) * 16
+    high_start = (size.rows - WIN_LAT + 1) * size.row_tokens // 16 * 16
+    high_rows = tokens - high_start
+    mid_start = size.row_tokens // 16 * 16
+    mid_rows = -(-(size.rows - 1) * size.row_tokens // 16) * 16 - mid_start
+
+    def rolled_index(start):
+        row, level, col = token_place(size, number(win, start))
         row, col = row - row_shift, col - col_shift
-        row = jnp.where(row < 0, row + size.rows, row)
         col = jnp.where(col < 0, col + size.cols, col)
-        return row * size.row_tokens + level * size.cols + col
-
-    square = (tokens, tokens)
-    roll_from = rolled_source(lax.broadcasted_iota(jnp.int32, (tokens, 1), 0))
-    roll_matrix = jnp.where(
-        roll_from == lax.broadcasted_iota(jnp.int32, square, 1), 1.0, 0.0
-    ).astype(BF16)
-    roll_to = rolled_source(lax.broadcasted_iota(jnp.int32, (1, tokens), 1))
-    unroll_matrix = jnp.where(
-        roll_to == lax.broadcasted_iota(jnp.int32, square, 0), 1.0, 0.0
-    ).astype(BF16)
-    row_of, unused, col_of = token_place(size, lax.broadcasted_iota(jnp.int32, (tokens, 1), 0))
-
-    def arrive(k, carry):
-        local_slot = jnp.logical_and(k == slot, jnp.logical_not(away))
-
-        @pl.when(local_slot)
-        def _():
-            own_block.wait()
-
-        @pl.when(jnp.logical_not(local_slot))
-        def _():
-            multicast(0, k).wait_recv()
-
-        return carry
-
-    lax.fori_loop(0, size.slots, arrive, 0)
+        return row, row * size.row_tokens + level * size.cols + col
+
+    first_row, first_index = rolled_index(0)
+    take_first = one_hot(
+        jnp.where(first_row < 0, first_index + tokens - high_start + low_rows, first_index),
+        low_rows + high_rows,
+    )
+    take_second = one_hot(rolled_index(win)[1] - mid_start, mid_rows)
+
+    row, level, col = token_place(size, number(tokens))
+    row, col = row + row_shift, col + col_shift
+    col = jnp.where(col >= size.cols, col - size.cols, col)
+    inner = level * size.cols + col
+    give_index = jnp.where(
+        row < WIN_LAT,
+        row * size.row_tokens + inner,
+        jnp.where(
+            row < 2 * WIN_LAT,
+            (row - WIN_LAT) * size.row_tokens + inner + win_pad,
+            (row - 2 * WIN_LAT) * size.row_tokens + inner + 2 * win_pad,
+        ),
+    )
+    give = one_hot(give_index, 2 * win_pad + low_rows)
+
+    def arrive(step):
+        def body(k, carry):
+            index = ((place + step) % share) * n_lat + k
+            local_slot = jnp.logical_and(index == slot, relay)
+
+            @pl.when(local_slot)
+            def _():
+                own_block.wait()
+
+            @pl.when(jnp.logical_not(local_slot))
+            def _():
+                block_copy(x_ref, index, own_send.at[0], (enc, lat, lon)).wait_recv()
+
+            @pl.when(relay)
+            def _():
+                for at, side in enumerate(sides):
+                    pass_copy(index, at * size.slots + index, (lat + side) % n_lat).start()
+
+            if passes_on is not None:
+
+                @pl.when(passes_on)
+                def _():
+                    pass_copy(index, index, opposite).start()
+
+            return carry
+
+        return body
+
+    for step in order:
+        lax.fori_loop(0, n_lat, arrive(step), 0)
 
     step_rows = tokens // 3
     blocks = lat_buf[...].reshape(size.slots * size.block_rows, size.width)
@@ -311,8 +383,6 @@
 
     next_lat, last_lat = (lat + 1) % n_lat, (lat + n_lat - 1) % n_lat
     next_lon, last_lon = (lon + 1) % n_lon, (lon + n_lon - 1) % n_lon
-    upper = tokens - packed
-
     def exchange(source, target, send, recv, k, *place):
         return pltpu.make_async_remote_copy(
             src_ref=source,
@@ -323,29 +393,40 @@
             device_id_type=MESH,
         )
 
-    lower_rows = halo.at[pl.ds(upper, packed)]
+    low_part = halo.at[pl.ds(0, low_rows)]
+    high_part = halo.at[pl.ds(high_start, high_rows)]
+    mid_part = halo.at[pl.ds(mid_start, mid_rows)]
     halo_copies = [
-        exchange(halo, halo_left, halo_send, halo_recv, 0, lat, next_lon),
-        exchange(lower_rows, halo_diag, halo_send, halo_recv, 1, next_lat, next_lon),
-        exchange(lower_rows, halo_up, halo_send, halo_recv, 2, next_lat, lon),
+        exchange(low_part, halo_left, halo_send, halo_recv, 0, lat, next_lon),
+        exchange(high_part, halo_diag, halo_send, halo_recv, 1, next_lat, next_lon),
+        exchange(high_part, halo_up, halo_send, halo_recv, 2, next_lat, lon),
+        exchange(mid_part, halo_right, halo_send, halo_recv, 3, lat, last_lon),
     ]
     for copy in halo_copies:
         copy.start()
     for copy in halo_copies:
         copy.wait_recv()
 
-    own_row = row_of < size.rows - row_shift
-    own_col = col_of < size.cols - col_shift
-    near = jnp.where(own_col, halo[...].astype(F32), halo_left[...].astype(F32))
-    far = jnp.where(own_col[upper:], halo_up[...].astype(F32), halo_diag[...].astype(F32))
-    spread = jnp.concatenate([near[:upper], jnp.where(own_row[upper:], near[upper:], far)], axis=0)
-    rolled = dot(roll_matrix, spread.astype(BF16))
-
-    win = size.half
+    split = size.cols - col_shift
+
+    def choose(condition, one, other):
+        return jnp.where(condition, one.astype(F32), other.astype(F32))
+
+    low = choose(column_of(low_rows) < split, halo[:low_rows, :], halo_left[...])
+    high = choose(column_of(high_rows, high_start) < split, halo_up[...], halo_diag[...])
+    middle = choose(
+        column_of(mid_rows, mid_start) < split,
+        halo_right[...],
+        halo[mid_start : mid_start + mid_rows, :],
+    )
+    windows = (
+        dot(take_first, jnp.concatenate([low, high], axis=0).astype(BF16)),
+        dot(take_second, middle.astype(BF16)),
+    )
+
     score_scale = HD ** (-0.5)
-    window_rows = WIN_LAT * size.row_tokens
-    for w in range(tokens // window_rows):
-        part = rolled[w * win : (w + 1) * win].astype(BF16)
+    for w in range(2):
+        part = windows[w].astype(BF16)
         queries, keys = part[:, :HD], part[:, HD : 2 * HD]
         values, grads = part[:, 2 * HD : 3 * HD], part[:, 3 * HD :]
         first = lat * size.rows + w * WIN_LAT
@@ -362,32 +443,41 @@
             grad_probs - jnp.sum(grad_probs * probs, axis=-1, keepdims=True)
         )
         grad_low = grad_scores.astype(BF16)
-        there = pl.ds(w * win, win)
+        there = pl.ds(w * win_pad, win)
         back_f[there, :HD] = dot(grad_low, keys) * score_scale
         back_f[there, HD : 2 * HD] = dot_ta(grad_low, queries) * score_scale
         back_f[there, 2 * HD : 3 * HD] = dot_ta(low, grads)
         back_f[there, 3 * HD :] = dot(low, values)
+        back_f[pl.ds(w * win_pad + win, win_pad - win), :] = jnp.zeros((win_pad - win, 4 * HD), F32)
     back[...] = back_f[...].astype(BF16)
 
-    upper_rows = back.at[pl.ds(0, packed)]
+    far_start = size.row_tokens // 16 * 16
+    far_rows = win_pad - far_start
+    early_part = back.at[pl.ds(0, low_rows)]
+    late_part = back.at[pl.ds(far_start, far_rows)]
+    second_part = back.at[pl.ds(win_pad, win_pad)]
     back_copies = [
-        exchange(back, back_right, back_send, back_recv, 0, lat, last_lon),
-        exchange(upper_rows, back_diag, back_send, back_recv, 1, last_lat, last_lon),
-        exchange(upper_rows, back_down, back_send, back_recv, 2, last_lat, lon),
+        exchange(late_part, back_right, back_send, back_recv, 0, lat, last_lon),
+        exchange(early_part, back_diag, back_send, back_recv, 1, last_lat, last_lon),
+        exchange(early_part, back_down, back_send, back_recv, 2, last_lat, lon),
+        exchange(second_part, back_left, back_send, back_recv, 3, lat, next_lon),
     ]
     for copy in back_copies:
         copy.start()
     for copy in back_copies:
         copy.wait_recv()
 
-    own_row = row_of >= row_shift
-    own_col = col_of >= col_shift
-    near = jnp.where(own_col, back[...].astype(F32), back_right[...].astype(F32))
-    far = jnp.where(own_col[:packed], back_down[...].astype(F32), back_diag[...].astype(F32))
-    spread = jnp.concatenate(
-        [jnp.where(own_row[:packed], near[:packed], far), near[packed:]], axis=0
-    )
-    own = dot(unroll_matrix, spread.astype(BF16)).astype(BF16)
+    here = back[...].astype(F32)
+    cover = jnp.concatenate(
+        [
+            here[:far_start],
+            choose(column_of(far_rows, far_start) >= col_shift, here[far_start:win_pad], back_right[...]),
+            choose(column_of(win_pad) >= col_shift, back_left[...], here[win_pad:]),
+            choose(column_of(low_rows) >= col_shift, back_down[...], back_diag[...]),
+        ],
+        axis=0,
+    )
+    own = dot(give, cover.astype(BF16)).astype(BF16)
     grad_rows, heads_out = own[:, : 3 * HD], own[:, 3 * HD :]
 
     head_part = dot_tb(grad_rows, wqkv_ref[...])
@@ -410,46 +500,76 @@
             message = pack_pair(values, odd, half)
             msg[2 * pair + odd] = jnp.concatenate([message, extra], axis=0).astype(BF16)
 
-    def head_copy(k, target):
+    later = tuple((place + step) % share for step in ((2, 1, 3, 0) if share == 4 else (1, 0)))
+
+    def group_copy(k, step):
+        target = (home + step) % n_lat
         return pltpu.make_async_remote_copy(
-            src_ref=msg.at[target],
-            dst_ref=msg_in.at[k],
-            send_sem=msg_send.at[k],
-            recv_sem=msg_recv.at[k],
-            device_id=(target, lat, lon),
+            src_ref=msg.at[target * share + later[k]],
+            dst_ref=msg_in.at[k, step],
+            send_sem=msg_send.at[k, step],
+            recv_sem=msg_recv.at[k, step],
+            device_id=(target * share + place, lat, lon),
             device_id_type=MESH,
         )
 
-    def send_head(k, carry):
-        head_copy(k, (enc + k) % n_enc).start()
-        return carry
-
-    lax.fori_loop(1, n_enc, send_head, 0)
-
-    grad[:, :, : 3 * HD] = (
+    group_copies = [
+        group_copy(k, step) for k in range(share) for step in ((2, 1, 3) if n_lat == 4 else (1,))
+    ]
+    for copy in group_copies:
+        copy.start()
+
+    grad[:, :, :, : 3 * HD] = (
         (dot_ta(hid_ref[...], grad_rows) * factor)
         .astype(BF16)
-        .reshape(group, size.chunk, 3 * HD)
-    )
-    grad[:, :, 3 * HD :] = (
-        (dot_ta(cot_ref[...], heads_out) * factor).astype(BF16).reshape(group, size.chunk, HD)
-    )
-
-    def grad_copy(k, target):
+        .reshape(n_lat, n_lon, size.chunk, 3 * HD)
+    )
+    grad[:, :, :, 3 * HD :] = (
+        (dot_ta(cot_ref[...], heads_out) * factor)
+        .astype(BF16)
+        .reshape(n_lat, n_lon, size.chunk, HD)
+    )
+
+    pairs = n_lat // 2
+    pair, core = lat // 2, lat % 2
+
+    def core_copy(k):
         return pltpu.make_async_remote_copy(
-            src_ref=grad.at[target],
+            src_ref=grad.at[((pair + k) % pairs) * 2 + 1 - core],
             dst_ref=grad_in.at[k],
             send_sem=grad_send.at[k],
             recv_sem=grad_recv.at[k],
-            device_id=(enc, target // n_lon, target % n_lon),
+            device_id=(enc, pair * 2 + 1 - core, lon),
             device_id_type=MESH,
         )
 
-    def send_grad(k, carry):
-        grad_copy(k, (member + k) % group).start()
-        return carry
-
-    lax.fori_loop(1, group, send_grad, 0)
+    def pair_copy():
+        return pltpu.make_async_remote_copy(
+            src_ref=mid,
+            dst_ref=mid_in,
+            send_sem=grad_send.at[pairs],
+            recv_sem=grad_recv.at[pairs],
+            device_id=(enc, ((pair + 1) % pairs) * 2 + core, lon),
+            device_id_type=MESH,
+        )
+
+    def line_copy(step):
+        target = (lon + step) % n_lon
+        return pltpu.make_async_remote_copy(
+            src_ref=total_out.at[target],
+            dst_ref=total_in.at[step],
+            send_sem=total_send.at[step],
+            recv_sem=total_recv.at[step],
+            device_id=(enc, lat, target),
+            device_id_type=MESH,
+        )
+
+    for k in reversed(range(pairs)):
+        core_copy(k).start()
+    if pairs == 2:
+        core_copy(1).wait_recv()
+        mid[...] = (grad[(1 - pair) * 2 + core].astype(F32) + grad_in[1].astype(F32)).astype(BF16)
+        pair_copy().start()
 
     columns = pl.ds(pl.multiple_of((enc // 2) * 128, 128), 128)
     odd = enc % 2 == 1
@@ -465,15 +585,48 @@
     cot_own = own_share(cot_ref[:, columns].astype(F32))
     inverse_own = side_by_side(inv_ref[...])
 
-    def take_head(k, total):
-        head_copy(k, enc).wait_recv()
-        return total + msg_in[k].astype(F32)
-
-    total = lax.fori_loop(1, n_enc, take_head, msg[enc].astype(F32))
+    def part_copy(k):
+        return pltpu.make_async_remote_copy(
+            src_ref=part_out.at[k],
+            dst_ref=part_in.at[k],
+            send_sem=part_send.at[k],
+            recv_sem=part_recv.at[k],
+            device_id=(home * share + later[k], lat, lon),
+            device_id_type=MESH,
+        )
+
+    def group_sum(k):
+        values = msg[home * share + later[k]].astype(F32)
+        for step in range(1, n_lat):
+            group_copy(k, step).wait_recv()
+            values = values + msg_in[k, step].astype(F32)
+        return values
+
+    def send_part(k):
+        part_out[k] = group_sum(k).astype(BF16)
+        part_copy(k).start()
+
+    send_part(0)
+    core_copy(0).wait_recv()
+    weight_sum = grad[lat].astype(F32) + grad_in[0].astype(F32)
+    if pairs == 2:
+        pair_copy().wait_recv()
+        weight_sum = weight_sum + mid_in[...].astype(F32)
+    total_out[...] = weight_sum.astype(BF16)
+    far_first = sorted(range(1, n_lon), key=lambda step: -min(step, n_lon - step))
+    for step in far_first:
+        line_copy(step).start()
+    for k in range(1, share - 1):
+        send_part(k)
+    total = group_sum(share - 1)
+    for k in range(share - 1):
+        part_copy(k).wait_recv()
+        total = total + part_in[k].astype(F32)
+
     token = lax.broadcasted_iota(jnp.int32, (tokens, 1), 0)
-    place = lax.broadcasted_iota(jnp.int32, (tokens, 128), 1)
+    lane = lax.broadcasted_iota(jnp.int32, (tokens, 128), 1)
     line = jnp.right_shift(token, 7)
-    pick = jnp.where(token - line * 128 == place, 1.0, 0.0)
+    pick = jnp.where(token - line * 128 == lane, 1.0, 0.0)
     means = lax.dot_general(
         pick,
         total[half:packed],
@@ -484,41 +637,55 @@
     which = lax.broadcasted_iota(jnp.int32, (tokens, 8), 1)
     mean_grad = jnp.sum(jnp.where(which == line, means, 0.0), axis=-1, keepdims=True)
     mean_cross = jnp.sum(jnp.where(which == line + 4, means, 0.0), axis=-1, keepdims=True)
-    latent_out[...] = (
-        cot_own
-        + inverse_own
-        * (total[:half] - side_by_side(mean_grad) - normed_own * side_by_side(mean_cross))
-    ).astype(BF16)
-
-    def take_grad(k, total):
-        grad_copy(k, member).wait_recv()
-        return total + grad_in[k].astype(F32)
-
-    weight_out[...] = lax.fori_loop(1, group, take_grad, grad[member].astype(F32))
+    latent = cot_own + inverse_own * (
+        total[:half] - side_by_side(mean_grad) - normed_own * side_by_side(mean_cross)
+    )
+    other = pltpu.roll(latent, HD, 1)
+    lines = size.rows * LEVELS // 2
+    for k in range(2 * lines):
+        start = (k % lines) * size.cols
+        values = (latent, other)[k // lines][start : start + size.cols, :HD]
+        latent_out[k % LEVELS, k // LEVELS] = values.astype(BF16)
+
+    weights = total_out[lon].astype(F32)
+    for step in reversed(far_first):
+        line_copy(step).wait_recv()
+        weights = weights + total_in[step].astype(F32)
+    qkv_out[...] = weights[:, : 3 * HD]
+    proj_out[...] = weights[:, 3 * HD :].T
 
     @pl.when(away)
     def _():
-        multicast(0, slot).wait_send()
-
-    def sent_block(k, carry):
-        multicast(k, slot).wait_send()
+        first_copy(0).wait_send()
+
+    for step in order[1:]:
+        first_copy(step).wait_send()
+
+    def passed(k, carry):
+        @pl.when(relay)
+        def _():
+            for at, side in enumerate(sides):
+                pass_copy(k, at * size.slots + k, (lat + side) % n_lat).wait_send()
+
+        if passes_on is not None:
+
+            @pl.when(passes_on)
+            def _():
+                pass_copy(k, k, opposite).wait_send()
+
         return carry
 
-    lax.fori_loop(1, n_enc, sent_block, 0)
-    for copy in halo_copies + back_copies:
+    lax.fori_loop(0, size.slots, passed, 0)
+    for copy in halo_copies + back_copies + group_copies:
         copy.wait_send()
-
-    def sent_head(k, carry):
-        head_copy(k, (enc + k) % n_enc).wait_send()
-        return carry
-
-    lax.fori_loop(1, n_enc, sent_head, 0)
-
-    def sent_grad(k, carry):
-        grad_copy(k, (member + k) % group).wait_send()
-        return carry
-
-    lax.fori_loop(1, group, sent_grad, 0)
+    for k in range(share - 1):
+        part_copy(k).wait_send()
+    for k in range(pairs):
+        core_copy(k).wait_send()
+    if pairs == 2:
+        pair_copy().wait_send()
+    for step in far_first:
+        line_copy(step).wait_send()
 
 
 def layer(size, lat_shift, lon_shift, block, wqkv, proj, cot):
@@ -528,14 +695,19 @@
     factor = (tokens * size.group) ** (-0.5)
     wide = 4 * HD
     dma = pltpu.SemaphoreType.DMA
+    low = -(-(WIN_LAT - 1) * size.row_tokens // 16) * 16
+    high = tokens - (size.rows - WIN_LAT + 1) * size.row_tokens // 16 * 16
+    one_row = size.row_tokens // 16 * 16
+    middle = -(-(size.rows - 1) * size.row_tokens // 16) * 16 - one_row
     return pl.pallas_call(
         functools.partial(layer_kernel, size, factor),
         out_shape=(
-            jax.ShapeDtypeStruct((size.half, 128), BF16),
-            jax.ShapeDtypeStruct((size.chunk, wide), F32),
+            jax.ShapeDtypeStruct((LEVELS, size.rows, size.cols, HD), BF16),
+            jax.ShapeDtypeStruct((size.chunk, 3 * HD), F32),
+            jax.ShapeDtypeStruct((HD, size.chunk), F32),
         ),
         in_specs=[smem, smem] + [vmem] * 5,
-        out_specs=(vmem, vmem),
+        out_specs=(vmem, vmem, vmem),
         scratch_shapes=[
             pltpu.VMEM((size.slots, size.block_rows, size.width), BF16),
             pltpu.VMEM((tokens, size.width), F32),
@@ -543,28 +715,41 @@
             pltpu.VMEM((tokens, size.width), BF16),
             pltpu.VMEM((tokens, wide), F32),
             pltpu.VMEM((tokens, wide), BF16),
-            pltpu.VMEM((tokens, wide), BF16),
-            pltpu.VMEM((packed, wide), BF16),
-            pltpu.VMEM((packed, wide), BF16),
-            pltpu.VMEM((tokens, wide), F32),
-            pltpu.VMEM((tokens, wide), BF16),
-            pltpu.VMEM((tokens, wide), BF16),
-            pltpu.VMEM((packed, wide), BF16),
+            pltpu.VMEM((low, wide), BF16),
+            pltpu.VMEM((high, wide), BF16),
+            pltpu.VMEM((high, wide), BF16),
+            pltpu.VMEM((middle, wide), BF16),
+            pltpu.VMEM((2 * packed, wide), F32),
+            pltpu.VMEM((2 * packed, wide), BF16),
+            pltpu.VMEM((packed - one_row, wide), BF16),
+            pltpu.VMEM((low, wide), BF16),
+            pltpu.VMEM((low, wide), BF16),
             pltpu.VMEM((packed, wide), BF16),
             pltpu.VMEM((size.enc, packed, 128), BF16),
-            pltpu.VMEM((size.enc, packed, 128), BF16),
-            pltpu.VMEM((size.group, size.chunk, wide), BF16),
-            pltpu.VMEM((size.group, size.chunk, wide), BF16),
-            dma((size.enc,)),
+            pltpu.VMEM((size.share, size.lat, packed, 128), BF16),
+            pltpu.VMEM((size.share, packed, 128), BF16),
+            pltpu.VMEM((size.share, packed, 128), BF16),
+            pltpu.VMEM((size.lat, size.lon, size.chunk, wide), BF16),
+            pltpu.VMEM((size.lat // 2, size.lon, size.chunk, wide), BF16),
+            pltpu.VMEM((size.lon, size.chunk, wide), BF16),
+            pltpu.VMEM((size.lon, size.chunk, wide), BF16),
+            pltpu.VMEM((size.lon, size.chunk, wide), BF16),
+            pltpu.VMEM((size.lon, size.chunk, wide), BF16),
+            dma((size.share,)),
+            dma((2 * size.slots,)),
             dma((size.slots,)),
-            dma((3,)),
-            dma((3,)),
-            dma((3,)),
-            dma((3,)),
-            dma((size.enc,)),
-            dma((size.enc,)),
-            dma((size.group,)),
-            dma((size.group,)),
+            dma((4,)),
+            dma((4,)),
+            dma((4,)),
+            dma((4,)),
+            dma((size.share, size.lat)),
+            dma((size.share, size.lat)),
+            dma((size.share,)),
+            dma((size.share,)),
+            dma((size.lat,)),
+            dma((size.lat,)),
+            dma((size.lon,)),
+            dma((size.lon,)),
         ],
         compiler_params=pltpu.CompilerParams(
             collective_id=0, has_side_effects=True, vmem_limit_bytes=56 * 1024 * 1024
@@ -576,12 +761,7 @@
     block = latent_band.reshape(size.block_tokens, size.width)
     block = jnp.pad(block, ((0, size.block_rows - size.block_tokens), (0, 0)))
     cot = cotangent.transpose(1, 0, 2, 3).reshape(size.tokens, size.width)
-    packed_latent, weights = layer(
-        size, lat_shift, lon_shift, block, qkv_weight, proj_weight, cot
-    )
-    latent = packed_latent.reshape(size.half, 2, HD).transpose(1, 0, 2)
-    latent = latent.reshape(size.rows, LEVELS, size.cols, HD).transpose(1, 0, 2, 3)
-    return latent, weights[:, : 3 * HD], weights[:, 3 * HD :].T
+    return layer(size, lat_shift, lon_shift, block, qkv_weight, proj_weight, cot)
 
 
 def local(

time: 128 us -> 99.5 us (0.78)
  Pallas kernels: 101 us -> 72.9 us
    pallas_call x1, Pallas kernels: 101 us -> 72.9 us  [layer(): pl.pallas_call(functools.partial(layer_kernel, size, factor), out_shape=(...]
    transpose x2 -> x0, local copies, waits for them, and re-layouts: 1.51 us -> none  [the longest x1 1.39 us: layer_part(): return (latent, weights[:, :3 * HD], weights[:, 3 * HD:].T)]
where the time goes in v2:
time: 99.5 us; the launch traced here: 99.2 us
  Pallas kernels  72.9 us (73%)
  local copies, waits for them, and re-layouts  12.2 us (12%)
  matrix products  9.95 us (10%)
  between operations  2.16 us (2%)
  other arithmetic  1.93 us (2%)
    pallas_call x1, Pallas kernels, layer(): pl.pallas_call(functools.partial(layer_kernel, size, factor), out_shape=(...  72.9 us
    unnamed x15, local copies, waits for them, and re-layouts  3.99 us
    dot_general x1, matrix products, merge_patches(): jnp.dot(merge_in.reshape(-1, 4 * width), merge_weight, preferred_element_...  3.15 us
    dot_general x1, matrix products, encode(): jnp.einsum('mhc,plhc->phml', queries, key_rows, preferred_element_type=jn...  2.36 us

profile of v2, /device:TPU:1, one launch (start us, length us, event | category | flops | bytes accessed | tf_op | source)
XLA Modules:
  0.0 99.2 jit_solution(16856636831816081521)
XLA Ops:
  0.6 0.8 convert_element_type.56
  1.5 1.0 %fusion.34 = f32[36,512]{1,0:T(8,128)S(1)} fusion(bf16[36,100]{1,0:T(8,128)(2,1)S(1)} %convert_element_type.57, bf16[100,512]{1,0:T(8,128)(2,1)} %param.20), kind=kOutput, calls=%fused_computation.35 | convolution fusion | flops 3686400 | bytes 183328 | tf_op jit(solution)/shard_map/dot_general | solution.py:48
  2.5 1.8 %fusion.32 = (f32[36,13]{0,1:T(8,128)S(1)}, f32[36,13,512]{2,0,1:T(8,128)S(1)}) fusion(f32[36,512]{1,0:T(8,128)S(1)} %fusion.34, f32[13,512]{1,0:T(8,128)} %param.21, bf16[500,512]{1,0:T(8,128)(2,1)} %param.19, bf16[36,13,500]{2,1,0:T(8,128)(2,1)} %bitcast.36), kind=kOutput, calls=%fused_computation.33 | convolution fusion | flops 240334384 | bytes 2040688 | tf_op jit(solution)/shard_map/dot_general | solution.py:44
  4.3 0.3 multiply_reduce_fusion
  4.6 0.2 multiply_convert_fusion
  4.9 0.2 copy.29
  5.0 0.2 reshape.101
  5.2 0.4 convolution_convert_fusion
  5.7 1.0 %reshape.103 = bf16[36,13,16,32]{3,2,1,0:T(8,128)(2,1)S(1)} reshape(bf16[468,512]{1,0:T(8,128)(2,1)S(1)} %convolution_convert_fusion) | data formatting | bytes 958464 | tf_op jit(solution)/shard_map/reshape | solution.py:60
  6.7 0.1 reshape.104
  6.9 2.4 %fusion.33 = (f32[36,16,3]{0,2,1:T(4,128)S(1)}, f32[36,16,3,13]{0,2,3,1:T(4,128)S(1)}) fusion(bf16[3,16,32,1]{2,1,0,3:T(8,128)(2,1)S(1)} %bitcast.35, bf16[36,13,16,32]{3,2,1,0:T(8,128)(2,1)S(1)} %reshape.103, pred[36,13]{0,1:T(8,128)(4,1)S(1)} %iota_compare_fusion), kind=kOutput, calls=%fused_computation.34 | convolution fusion | flops 1503360 | bytes 579540 | tf_op jit(solution)/shard_map/mhc,plhc->phml/dot_general | solution.py:65
  9.4 1.3 %copy.33 = bf16[36,16,3,13]{3,2,1,0:T(4,128)(2,1)S(1)} copy(bf16[36,16,3,13]{0,2,3,1:T(4,128)(2,1)S(1)} %divide_convert_fusion) | data formatting | bytes 89856 | tf_op jit(solution)/shard_map/convert_element_type | solution.py:70
  10.7 0.4 convolution_convert_fusion.1
  11.1 1.1 %reshape.102 = bf16[36,13,16,32]{3,2,1,0:T(8,128)(2,1)S(1)} reshape(bf16[468,512]{1,0:T(8,128)(2,1)S(1)} %convolution_convert_fusion.1) | data formatting | bytes 958464 | tf_op jit(solution)/shard_map/reshape | solution.py:61
  12.2 0.7 fusion.11
  13.0 0.3 reshape.111
  13.3 0.1 reshape.109
  13.5 0.2 fusion.31
  13.7 0.3 multiply_reduce_fusion.1
  14.0 0.1 rsqrt.21
  14.1 0.1 div.27
  14.2 0.1 copy.75
  14.3 0.2 reshape.107
  14.5 3.2 %convolution_convert_fusion.2 = bf16[27,1024]{1,0:T(8,128)(2,1)S(1)} fusion(bf16[2048,1024]{1,0:T(8,128)(2,1)} %param.25, f32[27,2048]{1,0:T(8,128)S(1)} %reshape.107, f32[27]{0:T(128)S(1)} %rsqrt.21, f32[27]{0:T(128)S(1)} %div.27), kind=kOutput, calls=%fused_computation.15 | convolution fusion | flops 113439744 | bytes 4471000 | tf_op jit(solution)/shard_map/dot_general | solution.py:85
  17.7 0.6 pad.4.x_ref
  18.3 0.1 copy.36
  18.4 1.1 %reshape.106.cot_ref = bf16[432,1024]{1,0:T(8,128)(2,1)} reshape(bf16[12,3,12,1024]{3,2,1,0:T(8,128)(2,1)S(1)} %copy.36) | data formatting | bytes 1769472 | tf_op jit(solution)/shard_map/reshape | solution.py:763
  19.6 1.0 %copy.37.wqkv_ref = bf16[1024,192]{1,0:T(8,128)(2,1)} copy(bf16[1024,192]{0,1:T(8,128)(2,1)S(1)} %copy-done.3) | data formatting | bytes 786432 | tf_op args[12]
  21.8 72.9 %shard_map.175 = (bf16[3,12,12,64]{3,2,1,0:T(8,128)(2,1)}, f32[32,192]{1,0:T(8,128)}, f32[64,32]{1,0:T(8,128)}) custom-call(s32[1]{0:T(128)S(6)} %copy.78.lat_shift, s32[1]{0:T(128)S(6)} %copy.79.lon_shift, bf16[32,1024]{1,0:T(8,128)(2,1)} %pad.4.x_ref, bf16[432,512]{1,0:T(8,128)(2,1)} %constant.20.clone.order_ref, bf16[1024,192]{1,0:T(8,128)(2,1)} %copy.37.wqkv_ref, ...), custom_call_target="tpu_custom_call" | custom-call | tf_op jit(solution)/shard_map/pallas_call | solution.py:702
  94.8 1.4 %copy.38 = f32[64,32]{0,1:T(8,128)} copy(f32[64,32]{1,0:T(8,128)} %get-tuple-element.8) | data formatting | bytes 16384 | tf_op jit(solution)/shard_map/pallas_call | solution.py:702
  96.2 1.6 %copy.80 = bf16[3,12,12,64]{3,2,1,0:T(8,128)(2,1)} copy(bf16[3,12,12,64]{3,2,1,0:T(8,128)(2,1)} %get-tuple-element.16) | data formatting | bytes 110592
  97.8 1.4 %copy.81 = f32[32,192]{1,0:T(8,128)} copy(f32[32,192]{1,0:T(8,128)} %get-tuple-element.17) | data formatting | bytes 49152
  (21 shorter events, 0.3 us)
Async XLA Ops:
  0.6 4.6 %copy-start = (bf16[512,512]{1,0:T(8,128)(2,1)S(1)}, bf16[512,512]{1,0:T(8,128)(2,1)}, u32[]{:S(2)}) copy-start(bf16[512,512]{1,0:T(8,128)(2,1)} %param.23) | copy-start | bytes 1572868
  5.6 1.1 %copy-start.5 = (bf16[3,512]{1,0:T(4,128)(2,1)S(1)}, bf16[3,512]{1,0:T(4,128)(2,1)}, u32[]{:S(2)}) copy-start(bf16[3,512]{1,0:T(4,128)(2,1)} %param.22) | copy-start | bytes 9220
  5.6 1.2 %copy-start.4 = (s32[6,6]{1,0:T(8,128)S(1)}, s32[6,6]{1,0:T(8,128)}, u32[]{:S(2)}) copy-start(s32[6,6]{1,0:T(8,128)} %param.18) | copy-start | bytes 436
  9.3 1.4 %copy-start.2 = (bf16[512,512]{1,0:T(8,128)(2,1)S(1)}, bf16[512,512]{1,0:T(8,128)(2,1)}, u32[]{:S(2)}) copy-start(bf16[512,512]{1,0:T(8,128)(2,1)} %param.24) | copy-start | bytes 1572868
  14.5 3.8 %copy-start.1 = (bf16[3,12,12,1024]{3,2,1,0:T(8,128)(2,1)S(1)}, bf16[3,12,12,1024]{3,2,1,0:T(8,128)(2,1)}, u32[]{:S(2)}) copy-start(bf16[3,12,12,1024]{3,2,1,0:T(8,128)(2,1)} %param.30) | copy-start | bytes 2654212
  18.4 1.1 %copy-start.3 = (bf16[1024,192]{0,1:T(8,128)(2,1)S(1)}, bf16[1024,192]{0,1:T(8,128)(2,1)}, u32[]{:S(2)}) copy-start(bf16[1024,192]{0,1:T(8,128)(2,1)} %param.28) | copy-start | bytes 1179652

commit v3 on v2

--- a/solution.py
+++ b/solution.py
@@ -13,6 +13,7 @@
 WIN_LON = 12
 HD = 64
 LEVELS = 3
+LINES = 16
 MESH = pl.DeviceIdType.MESH
 
 epsilon = 1e-05
@@ -28,69 +29,14 @@
     return (centred * inverse, inverse)
 
 
-def encode(
-    atmos,
-    land_sea,
-    level_count,
-    atm_weight,
-    land_weight,
-    level_embed,
-    latent_query,
-    key_weight,
-    value_weight,
-):
-    row_count, col_count, levels, pixels = atmos.shape
-    patches = row_count * col_count
-    embedded = jnp.dot(
-        atmos.reshape(patches * levels, pixels), atm_weight, preferred_element_type=jnp.float32
-    )
-    embedded = embedded.reshape(patches, levels, -1)
-    static = jnp.dot(
-        land_sea.reshape(patches, -1).astype(jnp.bfloat16),
-        land_weight,
-        preferred_element_type=jnp.float32,
-    )
-    embedded = embedded + level_embed[None, :, :] + static[:, None, :]
-    normed, unused_scale = layer_norm(embedded)
-    tokens = normed.astype(jnp.bfloat16).reshape(patches * levels, -1)
-    key_rows = jnp.dot(tokens, key_weight, preferred_element_type=jnp.float32).astype(jnp.bfloat16)
-    value_rows = jnp.dot(tokens, value_weight, preferred_element_type=jnp.float32).astype(
-        jnp.bfloat16
-    )
-    key_rows = key_rows.reshape(patches, levels, PHEADS, -1)
-    value_rows = value_rows.reshape(patches, levels, PHEADS, -1)
-    queries = latent_query.reshape(latent_query.shape[0], PHEADS, -1)
-    score_scale = key_rows.shape[-1] ** (-0.5)
-    scores = (
-        jnp.einsum("mhc,plhc->phml", queries, key_rows, preferred_element_type=jnp.float32)
-        * score_scale
-    )
-    present = jnp.arange(levels, dtype=jnp.int32)[None, :] < level_count.reshape(patches, 1)
-    weights = jnp.where(present[:, None, None, :], jnp.exp(scores), 0.0)
-    level_probs = (weights / jnp.sum(weights, axis=-1, keepdims=True)).astype(jnp.bfloat16)
-    attended = jnp.einsum(
-        "phml,plhc->pmhc", level_probs, value_rows, preferred_element_type=jnp.float32
-    )
-    attended = attended.astype(jnp.bfloat16).reshape(row_count, col_count, queries.shape[0], -1)
-    return attended.transpose(2, 0, 1, 3)
-
-
-def merge_patches(fine, merge_weight):
-    levels, row_count, col_count, width = fine.shape
-    grouped = fine.reshape(levels, row_count // 2, 2, col_count // 2, 2, width).transpose(
-        0, 1, 3, 4, 2, 5
-    )
-    grouped = grouped.reshape(levels, row_count // 2, col_count // 2, 4 * width)
-    merge_in = layer_norm(grouped.astype(jnp.float32))[0].astype(jnp.bfloat16)
-    merged = jnp.dot(
-        merge_in.reshape(-1, 4 * width), merge_weight, preferred_element_type=jnp.float32
-    ).astype(jnp.bfloat16)
-    return merged.reshape(levels, row_count // 2, col_count // 2, -1)
-
-
 class Sizes:
-    def __init__(self, enc, lat, lon, band, block, width):
+    def __init__(self, enc, lat, lon, fine_rows, fine_cols, width):
         self.enc, self.lat, self.lon = enc, lat, lon
+        band, block = fine_rows // 2, fine_cols // 2
+        self.fine_rows, self.fine_cols = fine_rows, fine_cols
+        self.patches = fine_rows * fine_cols
+        self.patch_rows = -(-self.patches // 8) * 8
+        self.fine_total = -(-LEVELS * self.patch_rows // 16) * 16
         self.band, self.block, self.width = band, block, width
         self.share = enc // lat
         self.rows, self.cols = self.share * band, lat * block
@@ -118,6 +64,18 @@
     return matrix
 
 
+def merge_order(size):
+    matrix = np.zeros((4 * size.block_rows, size.fine_total), np.float32)
+    for quadrant in range(4):
+        for level in range(LEVELS):
+            for i in range(size.band):
+                for j in range(size.block):
+                    patch = (2 * i + quadrant % 2) * size.fine_cols + 2 * j + quadrant // 2
+                    token = (level * size.band + i) * size.block + j
+                    matrix[quadrant * size.block_rows + token, level * size.patch_rows + patch] = 1.0
+    return matrix
+
+
 def token_place(size, token):
     row = ((token.astype(F32) + 0.5) * (1.0 / size.row_tokens)).astype(jnp.int32)
     rest = token - row * size.row_tokens
@@ -135,6 +93,105 @@
 
 def dot_ta(a, b):
     return lax.dot_general(a, b, (((0,), (0,)), ((), ())), preferred_element_type=F32)
+
+
+def encode_block(
+    size,
+    atmos_ref,
+    land_ref,
+    count_ref,
+    atm_weight_ref,
+    land_weight_ref,
+    level_ref,
+    query_ref,
+    key_ref,
+    value_ref,
+    select_ref,
+    merge_ref,
+    merge_ready,
+    atm_rows,
+    land_rows,
+    level_rows,
+    fine_rows,
+    block_ref,
+):
+    patches = size.patches
+    count, cols = patches * LINES, size.fine_cols
+    width = key_ref.shape[0]
+    atm_rows[...] = jnp.zeros_like(atm_rows)
+    land_rows[...] = jnp.zeros_like(land_rows)
+    level_rows[...] = jnp.zeros_like(level_rows)
+    fine_rows[...] = jnp.zeros_like(fine_rows)
+    for i in range(size.fine_rows):
+        land_rows[i * cols : (i + 1) * cols, :] = land_ref[i].astype(F32)
+        for j in range(cols):
+            atm_rows[i * cols + j, : atmos_ref.shape[2], :] = atmos_ref[i, j]
+    level_rows[: level_ref.shape[0], :] = level_ref[...]
+
+    token = lax.broadcasted_iota(jnp.int32, (count, 1), 0)
+    patch = jnp.right_shift(token, 4)
+    height = token - jnp.left_shift(patch, 4)
+    row = ((patch.astype(F32) + 0.5) * (1.0 / cols)).astype(jnp.int32)
+    col = patch - row * cols
+    spread = jnp.where(
+        patch == lax.broadcasted_iota(jnp.int32, (count, size.patch_rows), 1), 1.0, 0.0
+    ).astype(BF16)
+    in_row = jnp.where(
+        row == lax.broadcasted_iota(jnp.int32, (count, size.fine_rows), 1), 1.0, 0.0
+    ).astype(BF16)
+    counts = dot(in_row, count_ref[...].astype(F32).astype(BF16))
+    in_col = col == lax.broadcasted_iota(jnp.int32, (count, cols), 1)
+    limit = jnp.sum(jnp.where(in_col, counts, 0.0), axis=-1, keepdims=True)
+    present = height.astype(F32) < limit
+
+    land = dot(spread, land_rows[...].astype(BF16)).astype(BF16)
+    embedded = dot(atm_rows[...].reshape(count, atm_rows.shape[2]), atm_weight_ref[...])
+    embedded = embedded + dot(land, land_weight_ref[...])
+    embedded = embedded.reshape(patches, LINES, width) + level_rows[...][None]
+    tokens = layer_norm(embedded.reshape(count, width))[0].astype(BF16)
+    key_rows = dot(tokens, key_ref[...]).astype(BF16)
+    value_rows = dot(tokens, value_ref[...]).astype(BF16).astype(F32)
+
+    head_width = width // PHEADS
+    shape = (PHEADS, width)
+    lane = lax.broadcasted_iota(jnp.int32, shape, 1)
+    first = lax.broadcasted_iota(jnp.int32, shape, 0) * head_width
+    in_head = jnp.logical_and(lane >= first, lane < first + head_width)
+    queries = query_ref[...].astype(F32)
+    queries = jnp.concatenate(
+        [
+            jnp.where(in_head, jnp.broadcast_to(queries[m : m + 1], shape), 0.0)
+            for m in range(LEVELS)
+        ],
+        axis=0,
+    ).astype(BF16)
+    scores = dot_tb(key_rows, queries) * head_width ** (-0.5)
+    weights = jnp.where(present, jnp.exp(scores), 0.0).reshape(patches, LINES, LEVELS * PHEADS)
+    probs = weights / jnp.sum(weights, axis=1, keepdims=True)
+    probs = probs.reshape(count, LEVELS * PHEADS).astype(BF16)
+    shape = (LEVELS * PHEADS, LEVELS * width)
+    lane = lax.broadcasted_iota(jnp.int32, shape, 1)
+    first = lax.broadcasted_iota(jnp.int32, shape, 0) * head_width
+    widen = jnp.where(
+        jnp.logical_and(lane >= first, lane < first + head_width), 1.0, 0.0
+    ).astype(BF16)
+    for m in range(LEVELS):
+        wide = dot(probs, widen[:, m * width : (m + 1) * width])
+        attended = jnp.sum((wide * value_rows).reshape(patches, LINES, width), axis=1)
+        fine_rows[m * size.patch_rows : m * size.patch_rows + patches, :] = attended
+
+    merged = dot(select_ref[...], fine_rows[...].astype(BF16))
+    parts = [merged[q * size.block_rows : (q + 1) * size.block_rows] for q in range(4)]
+    centre = sum(jnp.sum(part, axis=-1, keepdims=True) for part in parts) * (0.25 / width)
+    parts = [part - centre for part in parts]
+    square = sum(jnp.sum(part * part, axis=-1, keepdims=True) for part in parts)
+    inverse = lax.rsqrt(square * (0.25 / width) + epsilon)
+    merge_ready()
+    block = sum(
+        dot((part * inverse).astype(BF16), merge_ref[q * width : (q + 1) * width, :])
+        for q, part in enumerate(parts)
+    )
+    block_ref[...] = block.astype(BF16)
 
 
 def pack_pair(values, odd, half):
@@ -150,14 +207,34 @@
     factor,
     lat_shift,
     lon_shift,
-    x_ref,
+    atmos_ref,
+    land_ref,
+    count_ref,
+    atm_weight_ref,
+    land_weight_ref,
+    level_ref,
+    query_ref,
+    key_ref,
+    value_ref,
+    cot_in,
+    select_hbm,
+    merge_hbm,
+    order_hbm,
+    wqkv_hbm,
+    proj_hbm,
+    latent_out,
+    weight_out,
+    select_ref,
+    merge_ref,
     order_ref,
     wqkv_ref,
     proj_ref,
     cot_ref,
-    latent_out,
-    qkv_out,
-    proj_out,
+    atm_rows,
+    land_rows,
+    level_rows,
+    fine_rows,
+    x_ref,
     lat_buf,
     normed_ref,
     inv_ref,
@@ -184,6 +261,7 @@
     mid_in,
     total_out,
     total_in,
+    load_sem,
     own_send,
     far_send,
     multi_recv,
@@ -206,6 +284,20 @@
     tokens, half, packed = size.tokens, size.half, size.packed
     away = home != lat
 
+    loads = [
+        pltpu.make_async_copy(source, target, load_sem.at[k])
+        for k, (source, target) in enumerate(
+            (
+                (select_hbm, select_ref),
+                (merge_hbm, merge_ref),
+                (proj_hbm, proj_ref),
+                (order_hbm, order_ref),
+                (wqkv_hbm, wqkv_ref),
+            )
+        )
+    ]
+    for load in loads:
+        load.start()
     barrier = pltpu.get_barrier_semaphore()
 
     def greet(*device):
@@ -239,6 +331,28 @@
         return carry
 
     lax.fori_loop(0, size.share * (n_lat - 1), greet_sources, 0)
+
+    loads[0].wait()
+    encode_block(
+        size,
+        atmos_ref,
+        land_ref,
+        count_ref,
+        atm_weight_ref,
+        land_weight_ref,
+        level_ref,
+        query_ref,
+        key_ref,
+        value_ref,
+        select_ref,
+        merge_ref,
+        loads[1].wait,
+        atm_rows,
+        land_rows,
+        level_rows,
+        fine_rows,
+        x_ref,
+    )
     expected = n_enc - 1 + group - 1 + size.share * (n_lat - 1)
     pl.semaphore_wait(barrier, jnp.where(away, expected + n_enc, expected))
 
@@ -284,6 +398,12 @@
     for step in order[1:]:
         first_copy(step).start()
 
+    for load in loads[2:]:
+        load.wait()
+    for k in range(size.rows * LEVELS):
+        rows = pl.ds(k * size.cols, size.cols)
+        normed_ref[rows, :] = cot_in[k % LEVELS, k // LEVELS].astype(F32)
+    cot_ref[...] = normed_ref[...].astype(BF16)
     halo_f[:, 3 * HD :] = dot_tb(cot_ref[...], proj_ref[...])
     row_shift, col_shift = lat_shift[0], lon_shift[0]
     win = size.half
@@ -375,7 +495,7 @@
         inv_ref[rows, :] = jnp.broadcast_to(inverse, (step_rows, 128))
         hidden = normed.astype(BF16)
         hid_ref[rows, :] = hidden
-        halo_f[rows, : 3 * HD] = dot(hidden, wqkv_ref[...])
+        halo_f[rows, : 3 * HD] = dot_tb(hidden, wqkv_ref[...])
         return carry
 
     lax.fori_loop(0, 3, normalise, 0)
@@ -480,7 +600,7 @@
     own = dot(give, cover.astype(BF16)).astype(BF16)
     grad_rows, heads_out = own[:, : 3 * HD], own[:, 3 * HD :]
 
-    head_part = dot_tb(grad_rows, wqkv_ref[...])
+    head_part = dot(grad_rows, wqkv_ref[...])
     ones = jnp.ones((8, size.width), BF16)
     sums = dot_tb(ones, head_part.astype(BF16))
     cross = dot_tb(ones, (head_part * normed_ref[...]).astype(BF16))
@@ -637,22 +757,15 @@
     which = lax.broadcasted_iota(jnp.int32, (tokens, 8), 1)
     mean_grad = jnp.sum(jnp.where(which == line, means, 0.0), axis=-1, keepdims=True)
     mean_cross = jnp.sum(jnp.where(which == line + 4, means, 0.0), axis=-1, keepdims=True)
-    latent = cot_own + inverse_own * (
+    latent_out[...] = cot_own + inverse_own * (
         total[:half] - side_by_side(mean_grad) - normed_own * side_by_side(mean_cross)
     )
-    other = pltpu.roll(latent, HD, 1)
-    lines = size.rows * LEVELS // 2
-    for k in range(2 * lines):
-        start = (k % lines) * size.cols
-        values = (latent, other)[k // lines][start : start + size.cols, :HD]
-        latent_out[k % LEVELS, k // LEVELS] = values.astype(BF16)
 
     weights = total_out[lon].astype(F32)
     for step in reversed(far_first):
         line_copy(step).wait_recv()
         weights = weights + total_in[step].astype(F32)
-    qkv_out[...] = weights[:, : 3 * HD]
-    proj_out[...] = weights[:, 3 * HD :].T
+    weight_out[...] = weights
 
     @pl.when(away)
     def _():
@@ -688,8 +801,35 @@
         line_copy(step).wait_send()
 
 
-def layer(size, lat_shift, lon_shift, block, wqkv, proj, cot):
+def finish_kernel(size, packed_ref, weight_ref, latent_out, qkv_out, proj_out):
+    latent = packed_ref[...]
+    other = pltpu.roll(latent, HD, 1)
+    lines = size.rows * LEVELS // 2
+    for k in range(2 * lines):
+        start = (k % lines) * size.cols
+        values = (latent, other)[k // lines][start : start + size.cols, :HD]
+        latent_out[k % LEVELS, k // LEVELS] = values.astype(BF16)
+    qkv_out[...] = weight_ref[:, : 3 * HD]
+    proj_out[...] = weight_ref[:, 3 * HD :]
+
+
+def finish(size, packed, weights):
+    vmem = pl.BlockSpec(memory_space=pltpu.VMEM)
+    return pl.pallas_call(
+        functools.partial(finish_kernel, size),
+        out_shape=(
+            jax.ShapeDtypeStruct((LEVELS, size.rows, size.cols, HD), BF16),
+            jax.ShapeDtypeStruct((size.chunk, 3 * HD), F32),
+            jax.ShapeDtypeStruct((size.chunk, HD), F32),
+        ),
+        in_specs=[vmem, vmem],
+        out_specs=(vmem, vmem, vmem),
+    )(packed, weights)
+
+
+def layer(size, lat_shift, lon_shift, arrays, merge, wqkv, proj):
     tokens, packed = size.tokens, size.packed
+    atmos, land, key = arrays[0], arrays[1], arrays[7]
     vmem = pl.BlockSpec(memory_space=pltpu.VMEM)
     smem = pl.BlockSpec(memory_space=pltpu.SMEM)
     factor = (tokens * size.group) ** (-0.5)
@@ -702,13 +842,23 @@
     return pl.pallas_call(
         functools.partial(layer_kernel, size, factor),
         out_shape=(
-            jax.ShapeDtypeStruct((LEVELS, size.rows, size.cols, HD), BF16),
-            jax.ShapeDtypeStruct((size.chunk, 3 * HD), F32),
-            jax.ShapeDtypeStruct((HD, size.chunk), F32),
+            jax.ShapeDtypeStruct((size.half, 128), F32),
+            jax.ShapeDtypeStruct((size.chunk, wide), F32),
         ),
-        in_specs=[smem, smem] + [vmem] * 5,
-        out_specs=(vmem, vmem, vmem),
+        in_specs=[smem, smem] + [vmem] * len(arrays) + [pl.BlockSpec(memory_space=pl.ANY)] * 5,
+        out_specs=(vmem, vmem),
         scratch_shapes=[
+            pltpu.VMEM((4 * size.block_rows, size.fine_total), BF16),
+            pltpu.VMEM(merge.shape, BF16),
+            pltpu.VMEM((tokens, size.slots * size.block_rows), BF16),
+            pltpu.VMEM(wqkv.shape, BF16),
+            pltpu.VMEM(proj.shape, BF16),
+            pltpu.VMEM((tokens, size.width), BF16),
+            pltpu.VMEM((size.patches, LINES, atmos.shape[3]), BF16),
+            pltpu.VMEM((size.patch_rows, land.shape[2]), F32),
+            pltpu.VMEM((LINES, key.shape[0]), F32),
+            pltpu.VMEM((size.fine_total, key.shape[0]), F32),
+            pltpu.VMEM((size.block_rows, size.width), BF16),
             pltpu.VMEM((size.slots, size.block_rows, size.width), BF16),
             pltpu.VMEM((tokens, size.width), F32),
             pltpu.VMEM((tokens, 128), F32),
@@ -735,6 +885,7 @@
             pltpu.VMEM((size.lon, size.chunk, wide), BF16),
             pltpu.VMEM((size.lon, size.chunk, wide), BF16),
             pltpu.VMEM((size.lon, size.chunk, wide), BF16),
+            dma((5,)),
             dma((size.share,)),
             dma((2 * size.slots,)),
             dma((size.slots,)),
@@ -754,14 +905,16 @@
         compiler_params=pltpu.CompilerParams(
             collective_id=0, has_side_effects=True, vmem_limit_bytes=56 * 1024 * 1024
         ),
-    )(lat_shift, lon_shift, block, jnp.asarray(block_order(size), BF16), wqkv, proj, cot)
-
-
-def layer_part(size, latent_band, lat_shift, lon_shift, qkv_weight, proj_weight, cotangent):
-    block = latent_band.reshape(size.block_tokens, size.width)
-    block = jnp.pad(block, ((0, size.block_rows - size.block_tokens), (0, 0)))
-    cot = cotangent.transpose(1, 0, 2, 3).reshape(size.tokens, size.width)
-    return layer(size, lat_shift, lon_shift, block, qkv_weight, proj_weight, cot)
+    )(
+        lat_shift,
+        lon_shift,
+        *arrays,
+        jnp.asarray(merge_order(size), BF16),
+        merge,
+        jnp.asarray(block_order(size), BF16),
+        wqkv,
+        proj,
+    )
 
 
 def local(
@@ -781,7 +934,15 @@
     proj_weight,
     cotangent,
 ):
-    fine_band = encode(
+    size = Sizes(
+        lax.axis_size("enc"),
+        lax.axis_size("lat"),
+        lax.axis_size("lon"),
+        atmos.shape[0],
+        atmos.shape[1],
+        merge_weight.shape[1],
+    )
+    arrays = (
         atmos,
         land_sea,
         level_count,
@@ -791,15 +952,13 @@
         latent_query,
         key_weight,
         value_weight,
-    )
-    latent_band = merge_patches(fine_band, merge_weight)
-    unused, band, block, width = latent_band.shape
-    size = Sizes(
-        lax.axis_size("enc"), lax.axis_size("lat"), lax.axis_size("lon"), band, block, width
-    )
-    return layer_part(
-        size, latent_band, lat_shift, lon_shift, qkv_weight, proj_weight, cotangent
-    )
+        cotangent,
+    )
+    packed, weights = layer(
+        size, lat_shift, lon_shift, arrays, merge_weight, qkv_weight.T, proj_weight
+    )
+    latent, grad_qkv, grad_proj = finish(size, packed, weights)
+    return latent, grad_qkv, grad_proj.T
 
 
 def solution(mesh):

time: 99.5 us -> 75.8 us (0.76)
  local copies, waits for them, and re-layouts: 12.2 us -> 0 us
  matrix products: 9.95 us -> 0 us
  other arithmetic: 1.93 us -> 0 us
    dot_general x7 -> x0, matrix products: 9.95 us -> none  [the longest x1 3.15 us: merge_patches(): jnp.dot(merge_in.reshape(-1, 4 * width), merge_weight, preferred_element_...]
    unnamed x15 -> x0, local copies, waits for them, and re-layouts: 3.99 us -> none
    reshape x5 -> x0, local copies, waits for them, and re-layouts: 3.48 us -> none  [the longest x1 1.12 us: layer_part(): cot = cotangent.transpose(1, 0, 2, 3).reshape(size.tokens, size.width)]
    convert_element_type x8 -> x0, local copies, waits for them, and re-layouts: 2.33 us -> none  [the longest x1 1.3 us: encode(): (weights / jnp.sum(weights, axis=-1, keepdims=True)).astype(jnp.bfloat16)]
    pallas_call x0 -> x1, Pallas kernels: none -> 1.65 us  [finish(): pl.pallas_call(functools.partial(finish_kernel, size), out_shape=(jax.Sha...]
    pallas_call x1 -> x0, local copies, waits for them, and re-layouts: 1.44 us -> none  [layer(): pl.pallas_call(functools.partial(layer_kernel, size, factor), out_shape=(...]
    convert_element_type x3 -> x0, other arithmetic: 1.09 us -> none  [the longest x1 0.8 us: encode(): land_sea.reshape(patches, -1).astype(jnp.bfloat16)]
where the time goes in v3:
time: 75.8 us; the launch traced here: 75.6 us
  Pallas kernels  73.7 us (97%)
  between operations  1.93 us (3%)
    pallas_call x1, Pallas kernels, layer(): pl.pallas_call(functools.partial(layer_kernel, size, factor), out_shape=(...  72 us
    pallas_call x1, Pallas kernels, finish(): pl.pallas_call(functools.partial(finish_kernel, size), out_shape=(jax.Sha...  1.65 us

profile of v3, /device:TPU:1, one launch (start us, length us, event | category | flops | bytes accessed | tf_op | source)
XLA Modules:
  0.0 75.6 jit_solution(9253132117964128478)
XLA Ops:
  1.9 72.0 %shard_map.184 = (f32[216,128]{1,0:T(8,128)}, f32[32,256]{1,0:T(8,128)}) custom-call(s32[1]{0:T(128)S(6)} %copy.20.lat_shift, s32[1]{0:T(128)S(6)} %copy.21.lon_shift, bf16[6,6,13,500]{3,2,1,0:T(8,128)(2,1)} %atmos_ref.1, s32[6,6,100]{2,1,0:T(8,128)} %land_ref.1, s32[6,6]{1,0:T(8,128)} %count_ref.1, bf16[500,512]{1,0:T(8,128)(2,1)} %atm_weight_ref.1, ...), custom_call_target="tpu_custom_call" | custom-call | tf_op jit(solution)/shard_map/pallas_call | solution.py:842
  74.0 1.7 %shard_map.185 = (bf16[3,12,12,64]{3,2,1,0:T(8,128)(2,1)}, f32[32,192]{1,0:T(8,128)}, f32[32,64]{1,0:T(8,128)}) custom-call(f32[216,128]{1,0:T(8,128)} %get-tuple-element.8.packed_ref, f32[32,256]{1,0:T(8,128)} %get-tuple-element.9.weight_ref), custom_call_target="tpu_custom_call" | custom-call | tf_op jit(solution)/shard_map/pallas_call | solution.py:818

commit v4 on v3

--- a/solution.py
+++ b/solution.py
@@ -108,7 +108,7 @@
     value_ref,
     select_ref,
     merge_ref,
-    merge_ready,
+    loads,
     atm_rows,
     land_rows,
     level_rows,
@@ -149,6 +149,8 @@
     embedded = embedded + dot(land, land_weight_ref[...])
     embedded = embedded.reshape(patches, LINES, width) + level_rows[...][None]
     tokens = layer_norm(embedded.reshape(count, width))[0].astype(BF16)
+    loads[0].wait()
+    loads[1].wait()
     key_rows = dot(tokens, key_ref[...]).astype(BF16)
     value_rows = dot(tokens, value_ref[...]).astype(BF16).astype(F32)
 
@@ -180,13 +182,14 @@
         attended = jnp.sum((wide * value_rows).reshape(patches, LINES, width), axis=1)
         fine_rows[m * size.patch_rows : m * size.patch_rows + patches, :] = attended
 
+    loads[2].wait()
     merged = dot(select_ref[...], fine_rows[...].astype(BF16))
     parts = [merged[q * size.block_rows : (q + 1) * size.block_rows] for q in range(4)]
     centre = sum(jnp.sum(part, axis=-1, keepdims=True) for part in parts) * (0.25 / width)
     parts = [part - centre for part in parts]
     square = sum(jnp.sum(part * part, axis=-1, keepdims=True) for part in parts)
     inverse = lax.rsqrt(square * (0.25 / width) + epsilon)
-    merge_ready()
+    loads[3].wait()
     block = sum(
         dot((part * inverse).astype(BF16), merge_ref[q * width : (q + 1) * width, :])
         for q, part in enumerate(parts)
@@ -214,10 +217,10 @@
     land_weight_ref,
     level_ref,
     query_ref,
-    key_ref,
-    value_ref,
     cot_in,
     select_hbm,
+    key_hbm,
+    value_hbm,
     merge_hbm,
     order_hbm,
     wqkv_hbm,
@@ -225,6 +228,8 @@
     latent_out,
     weight_out,
     select_ref,
+    key_ref,
+    value_ref,
     merge_ref,
     order_ref,
     wqkv_ref,
@@ -239,6 +244,8 @@
     normed_ref,
     inv_ref,
     hid_ref,
+    blocks_qkv,
+    products,
     halo_f,
     halo,
     halo_left,
@@ -288,6 +295,8 @@
         pltpu.make_async_copy(source, target, load_sem.at[k])
         for k, (source, target) in enumerate(
             (
+                (key_hbm, key_ref),
+                (value_hbm, value_ref),
                 (select_hbm, select_ref),
                 (merge_hbm, merge_ref),
                 (proj_hbm, proj_ref),
@@ -332,7 +341,6 @@
 
     lax.fori_loop(0, size.share * (n_lat - 1), greet_sources, 0)
 
-    loads[0].wait()
     encode_block(
         size,
         atmos_ref,
@@ -346,7 +354,7 @@
         value_ref,
         select_ref,
         merge_ref,
-        loads[1].wait,
+        loads,
         atm_rows,
         land_rows,
         level_rows,
@@ -398,7 +406,7 @@
     for step in order[1:]:
         first_copy(step).start()
 
-    for load in loads[2:]:
+    for load in loads[4:]:
         load.wait()
     for k in range(size.rows * LEVELS):
         rows = pl.ds(k * size.cols, size.cols)
@@ -481,25 +489,17 @@
 
         return body
 
+    band_rows = n_lat * size.block_rows
     for step in order:
         lax.fori_loop(0, n_lat, arrive(step), 0)
-
-    step_rows = tokens // 3
-    blocks = lat_buf[...].reshape(size.slots * size.block_rows, size.width)
-
-    def normalise(k, carry):
-        rows = pl.ds(pl.multiple_of(k * step_rows, 16), step_rows)
-        values = dot(order_ref[rows, :], blocks)
-        normed, inverse = layer_norm(values)
-        normed_ref[rows, :] = normed
-        inv_ref[rows, :] = jnp.broadcast_to(inverse, (step_rows, 128))
-        hidden = normed.astype(BF16)
-        hid_ref[rows, :] = hidden
-        halo_f[rows, : 3 * HD] = dot_tb(hidden, wqkv_ref[...])
-        return carry
-
-    lax.fori_loop(0, 3, normalise, 0)
+        band = (place + step) % share
+        values = lat_buf[pl.ds(band * n_lat, n_lat)].reshape(band_rows, size.width)
+        hidden = layer_norm(values.astype(F32))[0].astype(BF16)
+        rows = pl.ds(pl.multiple_of(band * band_rows, 16), band_rows)
+        blocks_qkv[rows, :] = dot_tb(hidden, wqkv_ref[...]).astype(BF16)
+    halo_f[:, : 3 * HD] = dot(order_ref[...], blocks_qkv[...])
     halo[...] = halo_f[...].astype(BF16)
+
 
     next_lat, last_lat = (lat + 1) % n_lat, (lat + n_lat - 1) % n_lat
     next_lon, last_lon = (lon + 1) % n_lon, (lon + n_lon - 1) % n_lon
@@ -524,6 +524,30 @@
     ]
     for copy in halo_copies:
         copy.start()
+
+    step_rows = tokens // 3
+    blocks = lat_buf[...].reshape(size.slots * size.block_rows, size.width)
+
+    def normalise(k, carry):
+        rows = pl.ds(pl.multiple_of(k * step_rows, 16), step_rows)
+        normed, inverse = layer_norm(dot(order_ref[rows, :], blocks))
+        normed_ref[rows, :] = normed
+        inv_ref[rows, :] = jnp.broadcast_to(inverse, (step_rows, 128))
+        hidden = normed.astype(BF16)
+        hid_ref[rows, :] = hidden
+        products[rows, :] = dot_tb(hidden, wqkv_ref[...])
+        return carry
+
+    lax.fori_loop(0, 3, normalise, 0)
+    ones = jnp.ones((8, size.width), BF16)
+    weight_sums = dot_tb(ones, wqkv_ref[...])
+    coarse = weight_sums.astype(BF16)
+    finer = (weight_sums - coarse.astype(F32)).astype(BF16)
+    index = lax.broadcasted_iota(jnp.int32, weight_sums.shape, 0)
+    weight_sums = jnp.where(
+        index == 0, coarse.astype(F32), jnp.where(index == 1, finer.astype(F32), 0.0)
+    ).astype(BF16)
+
     for copy in halo_copies:
         copy.wait_recv()
 
@@ -539,14 +563,10 @@
         halo_right[...],
         halo[mid_start : mid_start + mid_rows, :],
     )
-    windows = (
-        dot(take_first, jnp.concatenate([low, high], axis=0).astype(BF16)),
-        dot(take_second, middle.astype(BF16)),
-    )
-
     score_scale = HD ** (-0.5)
-    for w in range(2):
-        part = windows[w].astype(BF16)
+
+    def window(w, tokens_in, take):
+        part = dot(take, tokens_in.astype(BF16)).astype(BF16)
         queries, keys = part[:, :HD], part[:, HD : 2 * HD]
         values, grads = part[:, 2 * HD : 3 * HD], part[:, 3 * HD :]
         first = lat * size.rows + w * WIN_LAT
@@ -569,7 +589,8 @@
         back_f[there, 2 * HD : 3 * HD] = dot_ta(low, grads)
         back_f[there, 3 * HD :] = dot(low, values)
         back_f[pl.ds(w * win_pad + win, win_pad - win), :] = jnp.zeros((win_pad - win, 4 * HD), F32)
-    back[...] = back_f[...].astype(BF16)
+        whole = pl.ds(w * win_pad, win_pad)
+        back[whole, :] = back_f[whole, :].astype(BF16)
 
     far_start = size.row_tokens // 16 * 16
     far_rows = win_pad - far_start
@@ -582,8 +603,11 @@
         exchange(early_part, back_down, back_send, back_recv, 2, last_lat, lon),
         exchange(second_part, back_left, back_send, back_recv, 3, lat, next_lon),
     ]
-    for copy in back_copies:
+    window(0, jnp.concatenate([low, high], axis=0), take_first)
+    for copy in back_copies[:3]:
         copy.start()
+    window(1, middle, take_second)
+    back_copies[3].start()
     for copy in back_copies:
         copy.wait_recv()
 
@@ -600,10 +624,11 @@
     own = dot(give, cover.astype(BF16)).astype(BF16)
     grad_rows, heads_out = own[:, : 3 * HD], own[:, 3 * HD :]
 
-    head_part = dot(grad_rows, wqkv_ref[...])
-    ones = jnp.ones((8, size.width), BF16)
-    sums = dot_tb(ones, head_part.astype(BF16))
-    cross = dot_tb(ones, (head_part * normed_ref[...]).astype(BF16))
+    sums = dot_tb(weight_sums, grad_rows)
+    sums = sums + pltpu.roll(sums, 7, 0)
+    cross = dot_tb(
+        jnp.ones((8, 3 * HD), BF16), (grad_rows.astype(F32) * products[...]).astype(BF16)
+    )
     lanes = 4 * 128
     pad = jnp.zeros((8, lanes - tokens), F32)
     sums = jnp.concatenate([sums, pad], axis=1)
@@ -612,14 +637,8 @@
     extra = jnp.zeros((8, 128), F32)
     for k in range(4):
         columns = slice(k * 128, (k + 1) * 128)
-        extra = jnp.where(index == k, sums[:, columns], extra)
+        extra = jnp.where(index == k, jnp.broadcast_to(sums[:1, columns], (8, 128)), extra)
         extra = jnp.where(index == k + 4, cross[:, columns], extra)
-    for pair in range(n_enc // 2):
-        values = head_part[:, pair * 128 : (pair + 1) * 128]
-        for odd in range(2):
-            message = pack_pair(values, odd, half)
-            msg[2 * pair + odd] = jnp.concatenate([message, extra], axis=0).astype(BF16)
-
     later = tuple((place + step) % share for step in ((2, 1, 3, 0) if share == 4 else (1, 0)))
 
     def group_copy(k, step):
@@ -633,11 +652,20 @@
             device_id_type=MESH,
         )
 
-    group_copies = [
-        group_copy(k, step) for k in range(share) for step in ((2, 1, 3) if n_lat == 4 else (1,))
-    ]
-    for copy in group_copies:
-        copy.start()
+    group_copies = []
+    group_width = share * HD
+    for step in (2, 1, 3, 0) if n_lat == 4 else (1, 0):
+        target = (home + step) % n_lat
+        columns = pl.ds(pl.multiple_of(target * group_width, 128), group_width)
+        head_part = dot(grad_rows, wqkv_ref[:, columns])
+        for k in range(share):
+            values = head_part[:, k // 2 * 128 : (k // 2 + 1) * 128]
+            message = pack_pair(values, k % 2, half)
+            msg[target * share + k] = jnp.concatenate([message, extra], axis=0).astype(BF16)
+        if step > 0:
+            for k in range(share):
+                group_copies.append(group_copy(k, step))
+                group_copies[-1].start()
 
     grad[:, :, :, : 3 * HD] = (
         (dot_ta(hid_ref[...], grad_rows) * factor)
@@ -827,9 +855,9 @@
     )(packed, weights)
 
 
-def layer(size, lat_shift, lon_shift, arrays, merge, wqkv, proj):
+def layer(size, lat_shift, lon_shift, arrays, key, value, merge, wqkv, proj):
     tokens, packed = size.tokens, size.packed
-    atmos, land, key = arrays[0], arrays[1], arrays[7]
+    atmos, land = arrays[0], arrays[1]
     vmem = pl.BlockSpec(memory_space=pltpu.VMEM)
     smem = pl.BlockSpec(memory_space=pltpu.SMEM)
     factor = (tokens * size.group) ** (-0.5)
@@ -845,10 +873,12 @@
             jax.ShapeDtypeStruct((size.half, 128), F32),
             jax.ShapeDtypeStruct((size.chunk, wide), F32),
         ),
-        in_specs=[smem, smem] + [vmem] * len(arrays) + [pl.BlockSpec(memory_space=pl.ANY)] * 5,
+        in_specs=[smem, smem] + [vmem] * len(arrays) + [pl.BlockSpec(memory_space=pl.ANY)] * 7,
         out_specs=(vmem, vmem),
         scratch_shapes=[
             pltpu.VMEM((4 * size.block_rows, size.fine_total), BF16),
+            pltpu.VMEM(key.shape, BF16),
+            pltpu.VMEM(key.shape, BF16),
             pltpu.VMEM(merge.shape, BF16),
             pltpu.VMEM((tokens, size.slots * size.block_rows), BF16),
             pltpu.VMEM(wqkv.shape, BF16),
@@ -863,6 +893,8 @@
             pltpu.VMEM((tokens, size.width), F32),
             pltpu.VMEM((tokens, 128), F32),
             pltpu.VMEM((tokens, size.width), BF16),
+            pltpu.VMEM((size.slots * size.block_rows, 3 * HD), BF16),
+            pltpu.VMEM((tokens, 3 * HD), F32),
             pltpu.VMEM((tokens, wide), F32),
             pltpu.VMEM((tokens, wide), BF16),
             pltpu.VMEM((low, wide), BF16),
@@ -885,7 +917,7 @@
             pltpu.VMEM((size.lon, size.chunk, wide), BF16),
             pltpu.VMEM((size.lon, size.chunk, wide), BF16),
             pltpu.VMEM((size.lon, size.chunk, wide), BF16),
-            dma((5,)),
+            dma((7,)),
             dma((size.share,)),
             dma((2 * size.slots,)),
             dma((size.slots,)),
@@ -910,6 +942,8 @@
         lon_shift,
         *arrays,
         jnp.asarray(merge_order(size), BF16),
+        key,
+        value,
         merge,
         jnp.asarray(block_order(size), BF16),
         wqkv,
@@ -950,12 +984,18 @@
         land_weight,
         level_embed,
         latent_query,
+        cotangent,
+    )
+    packed, weights = layer(
+        size,
+        lat_shift,
+        lon_shift,
+        arrays,
         key_weight,
         value_weight,
-        cotangent,
-    )
-    packed, weights = layer(
-        size, lat_shift, lon_shift, arrays, merge_weight, qkv_weight.T, proj_weight
+        merge_weight,
+        qkv_weight.T,
+        proj_weight,
     )
     latent, grad_qkv, grad_proj = finish(size, packed, weights)
     return latent, grad_qkv, grad_proj.T

time: 75.8 us -> 75.1 us (level); the launches traced: 75.6 us -> 74.1 us
  Pallas kernels: 73.7 us -> 72.1 us
    pallas_call x1, Pallas kernels: 72 us -> 70.5 us  [layer(): pl.pallas_call(functools.partial(layer_kernel, size, factor), out_shape=(...]
where the time goes in v4:
time: 75.1 us; the launch traced here: 74.1 us
  Pallas kernels  72.1 us (96%)
  between operations  1.93 us (3%)
    pallas_call x1, Pallas kernels, layer(): pl.pallas_call(functools.partial(layer_kernel, size, factor), out_shape=(...  70.5 us
    pallas_call x1, Pallas kernels, finish(): pl.pallas_call(functools.partial(finish_kernel, size), out_shape=(jax.Sha...  1.65 us

profile of v4, /device:TPU:1, one launch (start us, length us, event | category | flops | bytes accessed | tf_op | source)
XLA Modules:
  0.0 74.1 jit_solution(16798894654259999696)
XLA Ops:
  1.9 70.5 %shard_map.184 = (f32[216,128]{1,0:T(8,128)}, f32[32,256]{1,0:T(8,128)}) custom-call(s32[1]{0:T(128)S(6)} %copy.20.lat_shift, s32[1]{0:T(128)S(6)} %copy.21.lon_shift, bf16[6,6,13,500]{3,2,1,0:T(8,128)(2,1)} %atmos_ref.1, s32[6,6,100]{2,1,0:T(8,128)} %land_ref.1, s32[6,6]{1,0:T(8,128)} %count_ref.1, bf16[500,512]{1,0:T(8,128)(2,1)} %atm_weight_ref.1, ...), custom_call_target="tpu_custom_call" | custom-call | tf_op jit(solution)/shard_map/pallas_call | solution.py:870
  72.4 1.7 %shard_map.185 = (bf16[3,12,12,64]{3,2,1,0:T(8,128)(2,1)}, f32[32,192]{1,0:T(8,128)}, f32[32,64]{1,0:T(8,128)}) custom-call(f32[216,128]{1,0:T(8,128)} %get-tuple-element.8.packed_ref, f32[32,256]{1,0:T(8,128)} %get-tuple-element.9.weight_ref), custom_call_target="tpu_custom_call" | custom-call | tf_op jit(solution)/shard_map/pallas_call | solution.py:846

commit v5 on v4

--- a/solution.py
+++ b/solution.py
@@ -284,6 +284,15 @@
     grad_recv,
     total_send,
     total_recv,
+    sums_out,
+    sums_in,
+    sums_send,
+    sums_recv,
+    rest_in,
+    rest_out,
+    rest_part,
+    rest_send,
+    rest_recv,
 ):
     enc, lat, lon = lax.axis_index("enc"), lax.axis_index("lat"), lax.axis_index("lon")
     n_enc, n_lat, n_lon, group = size.enc, size.lat, size.lon, size.group
@@ -312,34 +321,36 @@
     def greet(*device):
         pl.semaphore_signal(barrier, inc=1, device_id=device, device_id_type=MESH)
 
-    def greet_heads(k, carry):
-        greet((enc + k) % n_enc, lat, lon)
+    share = size.share
+    place = enc % share
+    next_lat, last_lat = (lat + 1) % n_lat, (lat + n_lat - 1) % n_lat
+    next_lon, last_lon = (lon + 1) % n_lon, (lon + n_lon - 1) % n_lon
+    for step in range(1, n_lat):
+        greet(((home + step) % n_lat) * share + place, lat, lon)
+        greet(enc, (lat + step) % n_lat, lon)
+    for step in range(1, share):
+        greet(home * share + (place + step) % share, lat, lon)
+    for step in range(1, n_lon):
+        greet(enc, lat, (lon + step) % n_lon)
+    greet(enc, next_lat, next_lon)
+    greet(enc, last_lat, last_lon)
+
+    def greet_targets(k, carry):
+        greet(home * share + k, home, lon)
         return carry
 
-    lax.fori_loop(1, n_enc, greet_heads, 0)
-    member = lat * n_lon + lon
-
-    def greet_tiles(k, carry):
-        other = (member + k) % group
-        greet(enc, other // n_lon, other % n_lon)
-        return carry
-
-    lax.fori_loop(1, group, greet_tiles, 0)
-
-    def greet_targets(k, carry):
-        greet(k, home, lon)
+    def greet_sources(k, carry):
+        for step in range(1, n_lat):
+            greet(home * share + k, (lat + step) % n_lat, lon)
         return carry
 
     @pl.when(away)
     def _():
-        lax.fori_loop(0, n_enc, greet_targets, 0)
-
-    def greet_sources(k, carry):
-        source = lat * size.share + k // (n_lat - 1)
-        greet(source, (lat + 1 + k % (n_lat - 1)) % n_lat, lon)
-        return carry
-
-    lax.fori_loop(0, size.share * (n_lat - 1), greet_sources, 0)
+        lax.fori_loop(0, share, greet_targets, 0)
+
+    @pl.when(jnp.logical_not(away))
+    def _():
+        lax.fori_loop(0, share, greet_sources, 0)
 
     encode_block(
         size,
@@ -361,11 +372,11 @@
         fine_rows,
         x_ref,
     )
-    expected = n_enc - 1 + group - 1 + size.share * (n_lat - 1)
-    pl.semaphore_wait(barrier, jnp.where(away, expected + n_enc, expected))
-
-    share = size.share
-    place = enc % share
+    expected = 2 * (n_lat - 1) + share - 1 + n_lon - 1 + 2
+    pl.semaphore_wait(
+        barrier, expected + jnp.where(away, share, share * (n_lat - 1)).astype(jnp.int32)
+    )
+
     slot = place * n_lat + lat
     order = (0, 1, 3, 2) if share == 4 else tuple(range(share))
     sides = (1, n_lat - 1) if n_lat > 2 else (1,)
@@ -501,8 +512,6 @@
     halo[...] = halo_f[...].astype(BF16)
 
 
-    next_lat, last_lat = (lat + 1) % n_lat, (lat + n_lat - 1) % n_lat
-    next_lon, last_lon = (lon + 1) % n_lon, (lon + n_lon - 1) % n_lon
     def exchange(source, target, send, recv, k, *place):
         return pltpu.make_async_remote_copy(
             src_ref=source,
@@ -576,7 +585,7 @@
         side_b = jnp.where(row_b + first < row_shift, 1, 0)
         scores = dot_tb(queries, keys) * score_scale
         weights = jnp.where(side_a == side_b, jnp.exp(scores), 0.0)
-        probs = weights / jnp.sum(weights, axis=-1, keepdims=True)
+        probs = weights * (1.0 / jnp.sum(weights, axis=-1, keepdims=True))
         low = probs.astype(BF16)
         grad_probs = dot_tb(grads, values)
         grad_scores = probs * (
@@ -608,6 +617,29 @@
         copy.start()
     window(1, middle, take_second)
     back_copies[3].start()
+
+    @pl.when(away)
+    def _():
+        first_copy(0).wait_send()
+
+    for step in order[1:]:
+        first_copy(step).wait_send()
+
+    def passed(k, carry):
+        @pl.when(relay)
+        def _():
+            for at, side in enumerate(sides):
+                pass_copy(k, at * size.slots + k, (lat + side) % n_lat).wait_send()
+
+        if passes_on is not None:
+
+            @pl.when(passes_on)
+            def _():
+                pass_copy(k, k, opposite).wait_send()
+
+        return carry
+
+    lax.fori_loop(0, size.slots, passed, 0)
     for copy in back_copies:
         copy.wait_recv()
 
@@ -639,12 +671,68 @@
         columns = slice(k * 128, (k + 1) * 128)
         extra = jnp.where(index == k, jnp.broadcast_to(sums[:1, columns], (8, 128)), extra)
         extra = jnp.where(index == k + 4, cross[:, columns], extra)
+    def sums_copy(step):
+        target = ((home + step) % n_lat) * share + place
+        return pltpu.make_async_remote_copy(
+            src_ref=sums_out.at[0],
+            dst_ref=sums_in.at[step - 1],
+            send_sem=sums_send.at[step - 1],
+            recv_sem=sums_recv.at[step - 1],
+            device_id=(target, lat, lon),
+            device_id_type=MESH,
+        )
+
+    def sums_part_copy(step):
+        target = home * share + (place + step) % share
+        return pltpu.make_async_remote_copy(
+            src_ref=sums_out.at[1],
+            dst_ref=sums_in.at[n_lat - 2 + step],
+            send_sem=sums_send.at[n_lat - 2 + step],
+            recv_sem=sums_recv.at[n_lat - 2 + step],
+            device_id=(target, lat, lon),
+            device_id_type=MESH,
+        )
+
+    filler = jnp.zeros((8, 128), F32)
+    sums_out[0] = jnp.concatenate([extra, filler], axis=0).astype(BF16)
+    sums_copies = [sums_copy(step) for step in range(1, n_lat)]
+    sums_copies += [sums_part_copy(step) for step in range(1, share)]
+    for copy in sums_copies[: n_lat - 1]:
+        copy.start()
+
     later = tuple((place + step) % share for step in ((2, 1, 3, 0) if share == 4 else (1, 0)))
+
+    most = packed - 48
+    rest = pl.ds(most, packed - most)
+    all_steps = (2, 1, 3, 0) if n_lat == 4 else (1, 0)
+
+    def rest_copy(step, near):
+        target = (place + near) % share
+        return pltpu.make_async_remote_copy(
+            src_ref=msg.at[((home + step) % n_lat) * share + target, rest],
+            dst_ref=rest_in.at[step, near],
+            send_sem=rest_send.at[step, near],
+            recv_sem=rest_recv.at[step, near],
+            device_id=(home * share + target, lat, lon),
+            device_id_type=MESH,
+        )
+
+    def rest_part_copy(step):
+        return pltpu.make_async_remote_copy(
+            src_ref=rest_out.at[step],
+            dst_ref=rest_part.at[step],
+            send_sem=rest_send.at[step, 0],
+            recv_sem=rest_recv.at[step, 0],
+            device_id=(((home + step) % n_lat) * share + place, lat, lon),
+            device_id_type=MESH,
+        )
+
+    rest_copies = []
 
     def group_copy(k, step):
         target = (home + step) % n_lat
         return pltpu.make_async_remote_copy(
-            src_ref=msg.at[target * share + later[k]],
+            src_ref=msg.at[target * share + later[k], pl.ds(0, most)],
             dst_ref=msg_in.at[k, step],
             send_sem=msg_send.at[k, step],
             recv_sem=msg_recv.at[k, step],
@@ -654,18 +742,21 @@
 
     group_copies = []
     group_width = share * HD
-    for step in (2, 1, 3, 0) if n_lat == 4 else (1, 0):
+    for step in all_steps:
         target = (home + step) % n_lat
         columns = pl.ds(pl.multiple_of(target * group_width, 128), group_width)
         head_part = dot(grad_rows, wqkv_ref[:, columns])
         for k in range(share):
             values = head_part[:, k // 2 * 128 : (k // 2 + 1) * 128]
             message = pack_pair(values, k % 2, half)
-            msg[target * share + k] = jnp.concatenate([message, extra], axis=0).astype(BF16)
+            msg[target * share + k] = jnp.concatenate([message, filler], axis=0).astype(BF16)
         if step > 0:
             for k in range(share):
                 group_copies.append(group_copy(k, step))
                 group_copies[-1].start()
+        for near in range(1, share):
+            rest_copies.append(rest_copy(step, near))
+            rest_copies[-1].start()
 
     grad[:, :, :, : 3 * HD] = (
         (dot_ta(hid_ref[...], grad_rows) * factor)
@@ -714,10 +805,20 @@
 
     for k in reversed(range(pairs)):
         core_copy(k).start()
+    feature_sums = jnp.concatenate([extra, filler], axis=0)
+    for k in range(n_lat - 1):
+        sums_copies[k].wait_recv()
+        feature_sums = feature_sums + sums_in[k].astype(F32)
+    sums_out[1] = feature_sums.astype(BF16)
+    for copy in sums_copies[n_lat - 1 :]:
+        copy.start()
     if pairs == 2:
         core_copy(1).wait_recv()
         mid[...] = (grad[(1 - pair) * 2 + core].astype(F32) + grad_in[1].astype(F32)).astype(BF16)
         pair_copy().start()
+
+    for copy in halo_copies + back_copies:
+        copy.wait_send()
 
     columns = pl.ds(pl.multiple_of((enc // 2) * 128, 128), 128)
     odd = enc % 2 == 1
@@ -744,7 +845,7 @@
         )
 
     def group_sum(k):
-        values = msg[home * share + later[k]].astype(F32)
+        values = msg[home * share + later[k], :most].astype(F32)
         for step in range(1, n_lat):
             group_copy(k, step).wait_recv()
             values = values + msg_in[k, step].astype(F32)
@@ -754,7 +855,38 @@
         part_out[k] = group_sum(k).astype(BF16)
         part_copy(k).start()
 
+    for k in range(n_lat - 1, len(sums_copies)):
+        sums_copies[k].wait_recv()
+        feature_sums = feature_sums + sums_in[k].astype(F32)
+    feature_sums = feature_sums[:8]
+    token = lax.broadcasted_iota(jnp.int32, (tokens, 1), 0)
+    lane = lax.broadcasted_iota(jnp.int32, (tokens, 128), 1)
+    line = jnp.right_shift(token, 7)
+    pick = jnp.where(token - line * 128 == lane, 1.0, 0.0)
+    means = lax.dot_general(
+        pick,
+        feature_sums,
+        (((1,), (1,)), ((), ())),
+        precision=lax.Precision.HIGHEST,
+        preferred_element_type=F32,
+    ) * (1.0 / size.width)
+    which = lax.broadcasted_iota(jnp.int32, (tokens, 8), 1)
+    mean_grad = jnp.sum(jnp.where(which == line, means, 0.0), axis=-1, keepdims=True)
+    mean_cross = jnp.sum(jnp.where(which == line + 4, means, 0.0), axis=-1, keepdims=True)
+    mean_grad_own, mean_cross_own = side_by_side(mean_grad), side_by_side(mean_cross)
+    fixed = cot_own - inverse_own * (mean_grad_own + normed_own * mean_cross_own)
+
+    def rest_sum(step):
+        values = msg[((home + step) % n_lat) * share + place, most:].astype(F32)
+        for near in range(1, share):
+            rest_copy(step, near).wait_recv()
+            values = values + rest_in[step, near].astype(F32)
+        return values
+
     send_part(0)
+    for step in all_steps[:-1]:
+        rest_out[step] = rest_sum(step).astype(BF16)
+        rest_part_copy(step).start()
     core_copy(0).wait_recv()
     weight_sum = grad[lat].astype(F32) + grad_in[0].astype(F32)
     if pairs == 2:
@@ -767,27 +899,22 @@
     for k in range(1, share - 1):
         send_part(k)
     total = group_sum(share - 1)
+    for copy in group_copies + sums_copies + rest_copies:
+        copy.wait_send()
+    for k in range(pairs):
+        core_copy(k).wait_send()
+    if pairs == 2:
+        pair_copy().wait_send()
     for k in range(share - 1):
         part_copy(k).wait_recv()
         total = total + part_in[k].astype(F32)
-
-    token = lax.broadcasted_iota(jnp.int32, (tokens, 1), 0)
-    lane = lax.broadcasted_iota(jnp.int32, (tokens, 128), 1)
-    line = jnp.right_shift(token, 7)
-    pick = jnp.where(token - line * 128 == lane, 1.0, 0.0)
-    means = lax.dot_general(
-        pick,
-        total[half:packed],
-        (((1,), (1,)), ((), ())),
-        precision=lax.Precision.HIGHEST,
-        preferred_element_type=F32,
-    ) * (1.0 / size.width)
-    which = lax.broadcasted_iota(jnp.int32, (tokens, 8), 1)
-    mean_grad = jnp.sum(jnp.where(which == line, means, 0.0), axis=-1, keepdims=True)
-    mean_cross = jnp.sum(jnp.where(which == line + 4, means, 0.0), axis=-1, keepdims=True)
-    latent_out[...] = cot_own + inverse_own * (
-        total[:half] - side_by_side(mean_grad) - normed_own * side_by_side(mean_cross)
-    )
+    rest_total = rest_sum(0)
+    for step in all_steps[:-1]:
+        rest_part_copy(step).wait_recv()
+        rest_total = rest_total + rest_part[step].astype(F32)
+    total = jnp.concatenate([total, rest_total], axis=0)
+
+    latent_out[...] = fixed + inverse_own * total[:half]
 
     weights = total_out[lon].astype(F32)
     for step in reversed(far_first):
@@ -795,36 +922,10 @@
         weights = weights + total_in[step].astype(F32)
     weight_out[...] = weights
 
-    @pl.when(away)
-    def _():
-        first_copy(0).wait_send()
-
-    for step in order[1:]:
-        first_copy(step).wait_send()
-
-    def passed(k, carry):
-        @pl.when(relay)
-        def _():
-            for at, side in enumerate(sides):
-                pass_copy(k, at * size.slots + k, (lat + side) % n_lat).wait_send()
-
-        if passes_on is not None:
-
-            @pl.when(passes_on)
-            def _():
-                pass_copy(k, k, opposite).wait_send()
-
-        return carry
-
-    lax.fori_loop(0, size.slots, passed, 0)
-    for copy in halo_copies + back_copies + group_copies:
-        copy.wait_send()
     for k in range(share - 1):
         part_copy(k).wait_send()
-    for k in range(pairs):
-        core_copy(k).wait_send()
-    if pairs == 2:
-        pair_copy().wait_send()
+    for step in all_steps[:-1]:
+        rest_part_copy(step).wait_send()
     for step in far_first:
         line_copy(step).wait_send()
 
@@ -908,9 +1009,9 @@
             pltpu.VMEM((low, wide), BF16),
             pltpu.VMEM((packed, wide), BF16),
             pltpu.VMEM((size.enc, packed, 128), BF16),
-            pltpu.VMEM((size.share, size.lat, packed, 128), BF16),
-            pltpu.VMEM((size.share, packed, 128), BF16),
-            pltpu.VMEM((size.share, packed, 128), BF16),
+            pltpu.VMEM((size.share, size.lat, packed - 48, 128), BF16),
+            pltpu.VMEM((size.share, packed - 48, 128), BF16),
+            pltpu.VMEM((size.share, packed - 48, 128), BF16),
             pltpu.VMEM((size.lat, size.lon, size.chunk, wide), BF16),
             pltpu.VMEM((size.lat // 2, size.lon, size.chunk, wide), BF16),
             pltpu.VMEM((size.lon, size.chunk, wide), BF16),
@@ -933,6 +1034,15 @@
             dma((size.lat,)),
             dma((size.lon,)),
             dma((size.lon,)),
+            pltpu.VMEM((2, 16, 128), BF16),
+            pltpu.VMEM((size.lat + size.share - 2, 16, 128), BF16),
+            dma((size.lat + size.share - 2,)),
+            dma((size.lat + size.share - 2,)),
+            pltpu.VMEM((size.lat, size.share, 48, 128), BF16),
+            pltpu.VMEM((size.lat, 48, 128), BF16),
+            pltpu.VMEM((size.lat, 48, 128), BF16),
+            dma((size.lat, size.share)),
+            dma((size.lat, size.share)),
         ],
         compiler_params=pltpu.CompilerParams(
             collective_id=0, has_side_effects=True, vmem_limit_bytes=56 * 1024 * 1024

time: 75.1 us -> 74.5 us (level); the launches traced: 74.1 us -> 74.3 us
  no operation moved by 1% of the time
where the time goes in v5:
time: 74.5 us; the launch traced here: 74.3 us
  Pallas kernels  72.4 us (97%)
  between operations  1.93 us (3%)
    pallas_call x1, Pallas kernels, layer(): pl.pallas_call(functools.partial(layer_kernel, size, factor), out_shape=(...  70.8 us
    pallas_call x1, Pallas kernels, finish(): pl.pallas_call(functools.partial(finish_kernel, size), out_shape=(jax.Sha...  1.65 us

profile of v5, /device:TPU:1, one launch (start us, length us, event | category | flops | bytes accessed | tf_op | source)
XLA Modules:
  0.0 74.3 jit_solution(12349460879672557230)
XLA Ops:
  1.9 70.8 %shard_map.184 = (f32[216,128]{1,0:T(8,128)}, f32[32,256]{1,0:T(8,128)}) custom-call(s32[1]{0:T(128)S(6)} %copy.20.lat_shift, s32[1]{0:T(128)S(6)} %copy.21.lon_shift, bf16[6,6,13,500]{3,2,1,0:T(8,128)(2,1)} %atmos_ref.1, s32[6,6,100]{2,1,0:T(8,128)} %land_ref.1, s32[6,6]{1,0:T(8,128)} %count_ref.1, bf16[500,512]{1,0:T(8,128)(2,1)} %atm_weight_ref.1, ...), custom_call_target="tpu_custom_call" | custom-call | tf_op jit(solution)/shard_map/pallas_call | solution.py:971
  72.7 1.7 %shard_map.185 = (bf16[3,12,12,64]{3,2,1,0:T(8,128)(2,1)}, f32[32,192]{1,0:T(8,128)}, f32[32,64]{1,0:T(8,128)}) custom-call(f32[216,128]{1,0:T(8,128)} %get-tuple-element.8.packed_ref, f32[32,256]{1,0:T(8,128)} %get-tuple-element.9.weight_ref), custom_call_target="tpu_custom_call" | custom-call | tf_op jit(solution)/shard_map/pallas_call | solution.py:947

commit v6 on v5

--- a/solution.py
+++ b/solution.py
@@ -288,6 +288,8 @@
     sums_in,
     sums_send,
     sums_recv,
+    side_send,
+    side_recv,
     rest_in,
     rest_out,
     rest_part,
@@ -328,6 +330,7 @@
     for step in range(1, n_lat):
         greet(((home + step) % n_lat) * share + place, lat, lon)
         greet(enc, (lat + step) % n_lat, lon)
+        greet(((home + step) % n_lat) * share + place, home, lon)
     for step in range(1, share):
         greet(home * share + (place + step) % share, lat, lon)
     for step in range(1, n_lon):
@@ -344,9 +347,14 @@
             greet(home * share + k, (lat + step) % n_lat, lon)
         return carry
 
+    def greet_side(k, carry):
+        greet(lat * share + place, k, lon)
+        return carry
+
     @pl.when(away)
     def _():
         lax.fori_loop(0, share, greet_targets, 0)
+        lax.fori_loop(0, n_lat, greet_side, 0)
 
     @pl.when(jnp.logical_not(away))
     def _():
@@ -372,9 +380,9 @@
         fine_rows,
         x_ref,
     )
-    expected = 2 * (n_lat - 1) + share - 1 + n_lon - 1 + 2
+    expected = 3 * (n_lat - 1) + share - 1 + n_lon - 1 + 2
     pl.semaphore_wait(
-        barrier, expected + jnp.where(away, share, share * (n_lat - 1)).astype(jnp.int32)
+        barrier, expected + jnp.where(away, share + n_lat, share * (n_lat - 1)).astype(jnp.int32)
     )
 
     slot = place * n_lat + lat
@@ -387,17 +395,44 @@
         passes_on = None
     opposite = (lat + 2) % n_lat
 
+    main = pl.ds(0, size.width - 128)
+    side_part = pl.ds(size.width - 128, 128)
+
     def block_copy(source, k, send, target):
         return pltpu.make_async_remote_copy(
-            src_ref=source,
-            dst_ref=lat_buf.at[k],
+            src_ref=source.at[:, main],
+            dst_ref=lat_buf.at[k, :, main],
             send_sem=send,
             recv_sem=multi_recv.at[k],
             device_id=target,
             device_id_type=MESH,
         )
 
-    own_block = pltpu.make_async_copy(x_ref, lat_buf.at[slot], multi_recv.at[slot])
+    own_block = pltpu.make_async_copy(
+        x_ref.at[:, main], lat_buf.at[slot, :, main], multi_recv.at[slot]
+    )
+    own_side = pltpu.make_async_copy(
+        x_ref.at[:, side_part], lat_buf.at[slot, :, side_part], side_recv.at[slot]
+    )
+
+    def side_copy(source, k, send, target):
+        return pltpu.make_async_remote_copy(
+            src_ref=source.at[:, side_part],
+            dst_ref=lat_buf.at[k, :, side_part],
+            send_sem=send,
+            recv_sem=side_recv.at[k],
+            device_id=target,
+            device_id_type=MESH,
+        )
+
+    def side_first(step):
+        target = (((home + step) % n_lat) * share + place, home, lon)
+        return side_copy(x_ref, slot, side_send.at[step], target)
+
+    def side_pass(k, near):
+        index = place * n_lat + k
+        target = (home * share + (place + near) % share, lat, lon)
+        return side_copy(lat_buf.at[index], index, side_send.at[n_lat * near + k], target)
 
     def first_copy(step):
         target = (home * share + (place + step) % share, home, lon)
@@ -409,10 +444,15 @@
     @pl.when(relay)
     def _():
         own_block.start()
+        own_side.start()
 
     @pl.when(away)
     def _():
         first_copy(0).start()
+        side_first(0).start()
+
+    for step in range(1, n_lat):
+        side_first(step).start()
 
     for step in order[1:]:
         first_copy(step).start()
@@ -484,6 +524,18 @@
             @pl.when(jnp.logical_not(local_slot))
             def _():
                 block_copy(x_ref, index, own_send.at[0], (enc, lat, lon)).wait_recv()
+
+            @pl.when(local_slot)
+            def _():
+                own_side.wait()
+
+            @pl.when(jnp.logical_not(local_slot))
+            def _():
+                side_copy(x_ref, index, side_send.at[0], (enc, lat, lon)).wait_recv()
+
+            if step == 0:
+                for near in range(1, share):
+                    side_pass(k, near).start()
 
             @pl.when(relay)
             def _():
@@ -621,6 +673,13 @@
     @pl.when(away)
     def _():
         first_copy(0).wait_send()
+        side_first(0).wait_send()
+
+    for step in range(1, n_lat):
+        side_first(step).wait_send()
+    for near in range(1, share):
+        for k in range(n_lat):
+            side_pass(k, near).wait_send()
 
     for step in order[1:]:
         first_copy(step).wait_send()
@@ -1038,6 +1097,8 @@
             pltpu.VMEM((size.lat + size.share - 2, 16, 128), BF16),
             dma((size.lat + size.share - 2,)),
             dma((size.lat + size.share - 2,)),
+            dma((size.lat * size.share,)),
+            dma((size.slots,)),
             pltpu.VMEM((size.lat, size.share, 48, 128), BF16),
             pltpu.VMEM((size.lat, 48, 128), BF16),
             pltpu.VMEM((size.lat, 48, 128), BF16),

time: 74.5 us -> 74.4 us (level)
  no operation moved by 1% of the time
where the time goes in v6:
time: 74.4 us; the launch traced here: 74.2 us
  Pallas kernels  72.3 us (97%)
  between operations  1.94 us (3%)
    pallas_call x1, Pallas kernels, layer(): pl.pallas_call(functools.partial(layer_kernel, size, factor), out_shape=(...  70.7 us
    pallas_call x1, Pallas kernels, finish(): pl.pallas_call(functools.partial(finish_kernel, size), out_shape=(jax.Sha...  1.65 us

profile of v6, /device:TPU:1, one launch (start us, length us, event | category | flops | bytes accessed | tf_op | source)
XLA Modules:
  0.0 74.2 jit_solution(17231326548313008482)
XLA Ops:
  1.9 70.7 %shard_map.184 = (f32[216,128]{1,0:T(8,128)}, f32[32,256]{1,0:T(8,128)}) custom-call(s32[1]{0:T(128)S(6)} %copy.20.lat_shift, s32[1]{0:T(128)S(6)} %copy.21.lon_shift, bf16[6,6,13,500]{3,2,1,0:T(8,128)(2,1)} %atmos_ref.1, s32[6,6,100]{2,1,0:T(8,128)} %land_ref.1, s32[6,6]{1,0:T(8,128)} %count_ref.1, bf16[500,512]{1,0:T(8,128)(2,1)} %atm_weight_ref.1, ...), custom_call_target="tpu_custom_call" | custom-call | tf_op jit(solution)/shard_map/pallas_call | solution.py:1030
  72.6 1.7 %shard_map.185 = (bf16[3,12,12,64]{3,2,1,0:T(8,128)(2,1)}, f32[32,192]{1,0:T(8,128)}, f32[32,64]{1,0:T(8,128)}) custom-call(f32[216,128]{1,0:T(8,128)} %get-tuple-element.8.packed_ref, f32[32,256]{1,0:T(8,128)} %get-tuple-element.9.weight_ref), custom_call_target="tpu_custom_call" | custom-call | tf_op jit(solution)/shard_map/pallas_call | solution.py:1006
